TPU v7x, 32 devices: a whole 2x2x4 slice. The times are simulated.
32 devices in a mesh: seq: 2 (over y), rep: 4 (over z), tensor: 4 (over x, core).
Axes of the slice: x: 2, y: 2, z: 4, core: 2. Of those that a mesh axis runs over, the one named last changes fastest.
Arguments:
- key_value_rows: bfloat16 [4, 3072, 8, 256], P('rep', ('seq', 'tensor')), may hold values from -32 to 32
- queries: bfloat16 [4, 64, 64, 128], P('rep', None, 'tensor'), may hold values from -136 to 136
- w_comp: bfloat16 [2048, 512], replicated, may hold values from -0.125 to 0.125
- latent_gain: bfloat16 [512], replicated, may hold values from 0.099609375 to 1.8984375
- w_up: bfloat16 [8, 512, 256], P('tensor'), may hold values from -0.25 to 0.25
- w_out: bfloat16 [8192, 8192], P('tensor', 'seq'), may hold values from -0.0625 to 0.0625
- replica_order: int32 [4], replicated, may hold values from 0 to 3, each once
Outputs:
- decoded: bfloat16 [4, 64, 8192], P('rep', None, 'seq')
Inputs may be any that keep to these rules, and one draw needn't show every extreme that they name: replica_order is a permutation of the prompts.
All inputs are finite; a program needn't handle non-finite values.
Results may differ from a plain program's by a relative error of at most 0.01.
Values may be sent and summed in bfloat16 or wider, within the bound.
No kernel may reach another device: no remote copies, remote signals or barrier semaphores. Data moves between devices by JAX's collectives and lax.ppermute only.
A program may use at most 64 MiB of HBM per device.

v0:
```python
import jax
import jax.numpy as jnp
from jax import lax
from jax.sharding import PartitionSpec as P


def compress(rows, weight, gain):
    projected = jnp.dot(rows, weight, preferred_element_type=jnp.float32)
    scale = lax.rsqrt(jnp.mean(projected * projected, axis=-1, keepdims=True) + 1e-06)
    return (projected * scale * gain.astype(jnp.float32)[None]).astype(jnp.bfloat16)


def shards(key_value_rows, queries, w_comp, latent_gain, w_up, w_out, replica_order):
    here = lax.axis_index("rep")
    piece = lax.all_gather(queries, "rep", axis=0, tiled=True)
    chosen = replica_order == here
    picked = jnp.sum(jnp.where(chosen[:, None, None, None], piece.astype(jnp.float32), 0.0), axis=0)
    query = jnp.where(
        jnp.any(chosen), picked.astype(piece.dtype), jnp.zeros(queries.shape[1:], queries.dtype)
    )
    rows = key_value_rows[0]
    tok_rows = rows.shape[0]
    latent_state = compress(rows.reshape(tok_rows, -1), w_comp, latent_gain)
    local_groups = w_up.shape[0]
    complete_up_weight = lax.all_gather(w_up, "tensor", axis=0, tiled=True)
    lifted_every_group = jnp.einsum(
        "qf,kfy->qky", latent_state, complete_up_weight, preferred_element_type=jnp.float32
    ).astype(jnp.bfloat16)
    tensor_count = lax.axis_size("tensor")
    split = lifted_every_group.reshape(
        tok_rows, tensor_count, local_groups, lifted_every_group.shape[-1]
    )
    moved = lax.all_to_all(split, "tensor", split_axis=1, concat_axis=0, tiled=True)
    lifted = moved.reshape(-1, local_groups, lifted_every_group.shape[-1])
    head_size = query.shape[-1]
    new_count = query.shape[0]
    keys = lifted[..., :head_size]
    values = lifted[..., head_size:]
    grouped_heads = query.reshape(new_count, local_groups, -1, head_size)
    scores = jnp.einsum(
        "nghd,tgd->nght", grouped_heads, keys, preferred_element_type=jnp.float32
    ) * head_size ** (-0.5)
    top = lax.pmax(jnp.max(scores, axis=-1), "seq")
    expo = jnp.exp(scores - top[..., None])
    total = jnp.sum(expo, axis=-1)
    weights = expo.astype(jnp.bfloat16)
    summed = jnp.einsum("nght,tgd->nghd", weights, values, preferred_element_type=jnp.float32)
    summed, total = lax.psum((summed, total), "seq")
    attended_values = (summed / total[..., None]).astype(jnp.bfloat16).reshape(new_count, -1)
    partial_output = jnp.dot(attended_values, w_out, preferred_element_type=jnp.float32)
    mixed = lax.psum(partial_output, "tensor").astype(jnp.bfloat16)[None]
    wanted = replica_order[here]
    piece = lax.all_gather(mixed, "rep", axis=0, tiled=True)
    sources = lax.iota(jnp.int32, piece.shape[0])
    chosen = sources == wanted
    picked = jnp.sum(jnp.where(chosen[:, None, None], piece.astype(jnp.float32), 0.0), axis=0)
    reply = jnp.where(
        jnp.any(chosen), picked.astype(piece.dtype), jnp.zeros(mixed.shape[1:], mixed.dtype)
    )
    return reply[None]


def solution(mesh):
    placed = (
        P("rep", ("seq", "tensor"), None, None),
        P("rep", None, "tensor", None),
        P(),
        P(),
        P("tensor", None, None),
        P("tensor", "seq"),
        P(),
    )
    return jax.shard_map(
        shards, mesh=mesh, in_specs=placed, out_specs=P("rep", None, "seq"), check_vma=False
    )
```

profile of v0, /device:TPU:0, one launch (start us, length us, event | category | flops | bytes accessed | tf_op | source)
XLA Modules:
  0.0 201.9 jit_solution(11448450707385098056)
XLA Ops:
  6.5 0.0 copy-start
  6.5 0.0 copy-start.2
  6.5 0.0 all-gather.5.cloned.1.call-start
  6.5 0.7 all-gather.5.cloned.1.call-update
  7.3 0.0 all-gather.7.cloned.1.call-start
  7.3 0.7 all-gather.7.cloned.1.call-update
  8.0 1.9 copy.16
  9.9 0.0 copy-done.2
  9.9 0.0 copy-done
  9.9 1.1 multiply_reduce_fusion
  11.0 23.2 %all-gather.5.cloned.1.call-done = bf16[8,512,256]{2,1,0:T(8,128)(2,1)} async-done(((bf16[2,512,256]{2,1,0:T(8,128)(2,1)}), bf16[8,512,256]{2,1,0:T(8,128)(2,1)}) %all-gather.5.cloned.1.call-update) | async-done | bytes 2097168 | tf_op jit(solution)/shard_map/all_gather | solution.py:25
  34.2 0.0 copy-start.3
  34.2 3.8 %convolution_convert_fusion = bf16[384,8,256]{2,0,1:T(8,128)(2,1)} fusion(bf16[8,512,256]{2,1,0:T(8,128)(2,1)} %all-gather.5.cloned.1.call-done, f32[384,512]{1,0:T(8,128)S(1)} %get-tuple-element.8, f32[512]{0:T(512)S(1)} %convert_element_type.40, f32[384]{0:T(512)S(1)} %add_rsqrt_fusion), kind=kOutput, calls=%fused_computation.11 | convolution fusion | flops 806682624 | bytes 4460032 | tf_op jit(solution)/shard_map/qf,kfy->qky/dot_general | solution.py:26
  38.0 4.3 %all-to-all-start = ((bf16[384,4,2,256]{3,0,2,1:T(8,128)(2,1)}), bf16[384,4,2,256]{3,0,2,1:T(8,128)(2,1)}, u32[]{:S(2)}, u32[]{:S(2)}) async-start(bf16[384,4,2,256]{3,0,2,1:T(8,128)(2,1)} %bitcast.57), calls=%async_computation | async-start | bytes 3145728 | tf_op jit(solution)/shard_map/all_to_all | solution.py:33
  42.4 0.0 all-reduce.3.cloned.1.call-start
  42.4 0.0 copy-done.3
  42.4 0.6 fusion.22
  43.1 20.7 %all-gather.7.cloned.1.call-done = bf16[4,64,16,128]{3,2,1,0:T(8,128)(2,1)} async-done(((bf16[1,64,16,128]{3,2,1,0:T(8,128)(2,1)}), bf16[4,64,16,128]{3,2,1,0:T(8,128)(2,1)}) %all-gather.7.cloned.1.call-update) | async-done | bytes 1048592 | tf_op jit(solution)/shard_map/all_gather | solution.py:15
  63.8 1.5 select_reduce_fusion
  65.3 0.7 select_bitcast_fusion.1
  66.0 0.0 all-to-all-done
  66.0 1.5 copy.11
  67.5 0.0 copy-start.1
  67.5 3.6 %bitcast_reduce_fusion = (f32[64,2,8]{0,2,1:T(8,128)S(1)}, f32[2,1536,64,8]{1,2,3,0:T(8,128)}) fusion(bf16[64,2,8,128]{3,2,1,0:T(8,128)(2,1)S(1)} %select_bitcast_fusion.1, bf16[1536,2,256]{2,0,1:T(8,128)(2,1)S(1)} %bitcast.53), kind=kOutput, calls=%fused_computation.1 | convolution fusion | flops 405797888 | bytes 7344128 | tf_op jit(solution)/shard_map/nghd,tgd->nght/dot_general | solution.py:40
  71.1 0.0 copy-done.1
  71.2 5.0 %pmax.7 = f32[64,2,8]{0,2,1:T(8,128)S(1)} all-reduce(f32[64,2,8]{0,2,1:T(8,128)S(1)} %get-tuple-element.9), channel_id=1, replica_groups=mesh['seq'=2,'rep'=4,'tensor'=4] {'seq'}, use_global_device_ids=true, to_apply=%region_5.6 | all-reduce | flops 1024 | bytes 8192 | tf_op jit(solution)/shard_map/pmax | solution.py:43
  76.1 4.9 %fusion.8 = f32[64,2,8,128]{3,0,2,1:T(8,128)} fusion(f32[2,1536,64,8]{1,2,3,0:T(8,128)} %get-tuple-element.10, f32[64,2,8]{0,2,1:T(8,128)S(1)} %pmax.7, bf16[1536,2,256]{2,0,1:T(8,128)(2,1)} %bitcast.54), kind=kOutput, calls=%fused_computation.12 | convolution fusion | flops 407371776 | bytes 7606272 | tf_op jit(solution)/shard_map/nght,tgd->nghd/dot_general | solution.py:47
  81.0 0.0 all-reduce.3.cloned.1.call-update
  81.1 0.0 all-gather.9.cloned.1.call-start
  81.1 4.0 %fusion.1 = f32[64,2,8]{0,2,1:T(8,128)S(1)} fusion(f32[2,1536,64,8]{1,2,3,0:T(8,128)} %get-tuple-element.10, f32[64,2,8]{0,2,1:T(8,128)S(1)} %pmax.7), kind=kLoop, calls=%fused_computation.3 | loop fusion | flops 4717568 | bytes 6299648 | tf_op jit(solution)/shard_map/reduce_sum | solution.py:45
  85.1 5.1 %psum.22 = f32[64,2,8]{0,2,1:T(8,128)S(1)} all-reduce(f32[64,2,8]{0,2,1:T(8,128)S(1)} %fusion.1), channel_id=1, replica_groups=mesh['seq'=2,'rep'=4,'tensor'=4] {'seq'}, use_global_device_ids=true, to_apply=%region_8.9 | all-reduce | flops 1024 | bytes 8192 | tf_op jit(solution)/shard_map/psum | solution.py:48
  90.2 19.2 %all-reduce.3.cloned.1.call-done = f32[64,2,8,128]{3,0,2,1:T(8,128)} async-done(((f32[64,2,8,128]{3,0,2,1:T(8,128)}), f32[64,2,8,128]{3,0,2,1:T(8,128)}) %all-reduce.3.cloned.1.call-update) | async-done | bytes 524304 | tf_op jit(solution)/shard_map/psum | solution.py:48
  109.4 1.2 divide_convert_fusion
  110.7 0.2 copy.13
  110.8 8.8 %fusion.16 = f32[64,4096]{1,0:T(8,128)S(1)} fusion(bf16[2048,4096]{1,0:T(8,128)(2,1)} %param.12, bf16[8,8,16,128]{3,2,1,0:T(8,128)(2,1)S(1)} %bitcast.59), kind=kOutput, calls=%fused_computation.23 | convolution fusion | flops 1073741824 | bytes 18087936 | tf_op jit(solution)/shard_map/dot_general | solution.py:50
  119.6 26.9 %all-reduce.4 = bf16[64,4096]{1,0:T(8,128)(2,1)} all-reduce(f32[64,4096]{1,0:T(8,128)S(1)} %fusion.16), channel_id=1, replica_groups=mesh['seq'=2,'rep'=4,'tensor'=4] {'tensor'}, use_global_device_ids=true, to_apply=%region_9.10 | all-reduce | flops 262144 | bytes 1572864 | tf_op jit(solution)/shard_map/psum | solution.py:51
  146.5 0.0 all-gather.9.cloned.1.call-update
  146.6 0.6 dynamic_slice.3
  147.2 1.2 iota_compare_fusion
  148.4 43.4 %all-gather.9.cloned.1.call-done = bf16[256,4096]{1,0:T(8,128)(2,1)} async-done(((bf16[64,4096]{1,0:T(8,128)(2,1)}), bf16[256,4096]{1,0:T(8,128)(2,1)}) %all-gather.9.cloned.1.call-update) | async-done | bytes 2097168 | tf_op jit(solution)/shard_map/all_gather | solution.py:53
  191.8 2.1 %fusion.3 = bf16[64,4096]{1,0:T(8,128)(2,1)S(1)} fusion(bf16[4,64,4096]{2,1,0:T(8,128)(2,1)} %bitcast.55, pred[4]{0:T(512)(128)(4,1)S(1)} %get-tuple-element.11), kind=kLoop, calls=%fused_computation.6 | loop fusion | flops 2883584 | bytes 2621444 | tf_op jit(solution)/shard_map/reduce_sum | solution.py:56
  193.9 1.4 select_bitcast_fusion
  (2 shorter events, 0.0 us)
Async XLA Ops:
  6.5 3.4 %copy-start = (bf16[2048,512]{1,0:T(8,128)(2,1)S(1)}, bf16[2048,512]{1,0:T(8,128)(2,1)}, u32[]{:S(2)}) copy-start(bf16[2048,512]{1,0:T(8,128)(2,1)} %param.9) | copy-start | bytes 6291460
  6.5 3.4 %copy-start.2 = (bf16[512]{0:T(512)(128)(2,1)S(1)}, bf16[512]{0:T(512)(128)(2,1)}, u32[]{:S(2)}) copy-start(bf16[512]{0:T(512)(128)(2,1)} %param.10) | copy-start | bytes 3076
  6.5 27.7 %all-gather.5.cloned.1.call-start = ((), (), s32[]{:S(2)}) async-start(), calls=%async_computation.1 | async-start | bytes 2621440 | tf_op jit(solution)/shard_map/all_gather | solution.py:25
  7.3 56.5 %all-gather.7.cloned.1.call-start = ((), (), s32[]{:S(2)}) async-start(), calls=%async_computation.2 | async-start | bytes 1310720 | tf_op jit(solution)/shard_map/all_gather | solution.py:15
  34.2 8.2 %copy-start.3 = (s32[4]{0:T(128)S(1)}, s32[4]{0:T(128)}, u32[]{:S(2)}) copy-start(s32[4]{0:T(128)} %param.13) | copy-start | bytes 52
  38.0 27.9 %all-to-all-start = ((bf16[384,4,2,256]{3,0,2,1:T(8,128)(2,1)}), bf16[384,4,2,256]{3,0,2,1:T(8,128)(2,1)}, u32[]{:S(2)}, u32[]{:S(2)}) async-start(bf16[384,4,2,256]{3,0,2,1:T(8,128)(2,1)} %bitcast.57), calls=%async_computation | async-start | bytes 3145728 | tf_op jit(solution)/shard_map/all_to_all | solution.py:33
  42.4 67.0 %all-reduce.3.cloned.1.call-start = ((), (), s32[]{:S(2)}) async-start(), calls=%async_computation.3 | async-start | bytes 1048576 | tf_op jit(solution)/shard_map/psum | solution.py:48
  67.5 3.7 %copy-start.1 = (bf16[4,384,1,2,256]{4,1,0,3,2:T(8,128)(2,1)}, bf16[4,384,1,2,256]{4,1,0,3,2:T(8,128)(2,1)S(1)}, u32[]{:S(2)}) copy-start(bf16[4,384,1,2,256]{4,1,0,3,2:T(8,128)(2,1)S(1)} %copy.11) | copy-start | bytes 4718596
  81.1 110.8 %all-gather.9.cloned.1.call-start = ((), (), s32[]{:S(2)}) async-start(), calls=%async_computation.4 | async-start | bytes 2621440 | tf_op jit(solution)/shard_map/all_gather | solution.py:53
Sparse Core Ops, SparseCore 0:
  8.9 25.2 all-gather.4
  35.8 27.9 all-gather.6
  81.2 28.1 all-reduce.2
  146.7 45.0 all-gather.8
where the time goes:
time: 202 us
  waiting for transfers between devices  108 us (53%)
  blocking collectives  37 us (18%)
  matrix products  22.2 us (11%)
  between operations  13.2 us (7%)
  other arithmetic  12.8 us (6%)
  starting transfers between devices  4.46 us (2%)
  local copies, waits for them, and re-layouts  4.22 us (2%)
    all_gather x1, waiting for transfers between devices, shards(): piece = lax.all_gather(mixed, 'rep', axis=0, tiled=True)  43.4 us
    psum x1, blocking collectives, shards(): mixed = lax.psum(partial_output, 'tensor').astype(jnp.bfloat16)[None]  26.9 us
    all_gather x1, waiting for transfers between devices, shards(): complete_up_weight = lax.all_gather(w_up, 'tensor', axis=0, tiled=True)  23.2 us
    all_gather x1, waiting for transfers between devices, shards(): piece = lax.all_gather(queries, 'rep', axis=0, tiled=True)  20.7 us
    psum x1, waiting for transfers between devices, shards(): summed, total = lax.psum((summed, total), 'seq')  19.2 us
    dot_general x1, matrix products, shards(): jnp.dot(attended_values, w_out, preferred_element_type=jnp.float32)  8.78 us
    psum x1, blocking collectives, shards(): summed, total = lax.psum((summed, total), 'seq')  5.09 us
    pmax x1, blocking collectives, shards(): top = lax.pmax(jnp.max(scores, axis=-1), 'seq')  4.97 us
  transfers between devices with their start and end apart: 5, of which 4 were waited for; matrix products, arithmetic and copies ran while one was open for 8% of the time, Pallas kernels for 0%

commit v1 on v0

v1 whole, which is shorter than its diff:
```python
import itertools
import math

import jax
import jax.numpy as jnp
from jax import lax
from jax.experimental import pallas as pl
from jax.experimental.pallas import tpu as pltpu
from jax.sharding import PartitionSpec as P

BF16, F32 = jnp.bfloat16, jnp.float32
VMEM_BYTES = 48 * 1024 * 1024
IN_VMEM = pl.BlockSpec(memory_space=pltpu.VMEM)
IN_SMEM = pl.BlockSpec(memory_space=pltpu.SMEM)


def params():
    return pltpu.CompilerParams(vmem_limit_bytes=VMEM_BYTES)


def compress(rows, weight, gain):
    projected = jnp.dot(rows, weight, preferred_element_type=F32)
    scale = lax.rsqrt(jnp.mean(projected * projected, axis=-1, keepdims=True) + 1e-06)
    return (projected * scale * gain.astype(F32)[None]).astype(BF16)


def order_index(replica_order, orders):
    table = jnp.array(orders, jnp.int32)
    match = jnp.all(table == replica_order[None], axis=1)
    return jnp.sum(jnp.where(match, lax.iota(jnp.int32, len(orders)), 0))


def route(value, index, orders, back):
    def branch(order):
        pairs = [(p, r) if back else (r, p) for r, p in enumerate(order)]
        return lambda v: lax.ppermute(v, "rep", pairs)

    return lax.switch(index, [branch(o) for o in orders], value)


def swap(value, axis, bit):
    pairs = [(i, i ^ bit) for i in range(lax.axis_size(axis))]
    return lax.ppermute(value, axis, pairs)


def attend(latents, lift, query):
    head_size = query.shape[-1]
    coef = head_size ** (-0.5) * math.log2(math.e)
    scores, values = [], []
    for latent in latents:
        lifted = jnp.dot(latent, lift, preferred_element_type=F32).astype(BF16)
        scores.append(
            lax.dot_general(
                lifted[:, :head_size], query, (((1,), (1,)), ((), ())), preferred_element_type=F32
            )
        )
        values.append(lifted[:, head_size:])
    top = jnp.max(scores[0], axis=0, keepdims=True)
    for score in scores[1:]:
        top = jnp.maximum(top, jnp.max(score, axis=0, keepdims=True))
    total, summed = 0.0, 0.0
    for score, value in zip(scores, values):
        expo = jnp.exp2((score - top) * coef)
        total = total + jnp.sum(expo, axis=0, keepdims=True)
        summed = summed + lax.dot_general(
            value, expo.astype(BF16), (((0,), (0,)), ((), ())), preferred_element_type=F32
        )
    return summed, top, total


def merge(one, two, head_size):
    coef = head_size ** (-0.5) * math.log2(math.e)
    top = jnp.maximum(one[1], two[1])
    scale_one = jnp.exp2((one[1] - top) * coef)
    scale_two = jnp.exp2((two[1] - top) * coef)
    return (
        one[0] * scale_one + two[0] * scale_two,
        top,
        one[2] * scale_one + two[2] * scale_two,
    )


def unpack(state, head_size):
    return state[:head_size], state[head_size : head_size + 1], state[head_size + 4 : head_size + 5]


def store(ref, state, head_size):
    columns = state[0].shape[1]
    ref[:head_size, :] = state[0]
    ref[head_size : head_size + 4, :] = jnp.broadcast_to(state[1], (4, columns))
    ref[head_size + 4 :, :] = jnp.broadcast_to(state[2], (4, columns))


def first_kernel(place_ref, lat_a, lat_b, lift_ref, query_ref, out_ref):
    head_size = query_ref.shape[-1]
    mine = place_ref[0]
    for slot, group in enumerate((1 - mine, mine)):
        state = attend((lat_a[...], lat_b[...]), lift_ref[group], query_ref[group])
        store(out_ref.at[slot], state, head_size)


def later_kernel(slot, place_ref, lat_a, lat_b, lift_ref, query_ref, before_ref, out_ref):
    head_size = query_ref.shape[-1]
    mine = place_ref[0]
    group = mine if slot else 1 - mine
    state = attend((lat_a[...], lat_b[...]), lift_ref[group], query_ref[group])
    store(out_ref, merge(unpack(before_ref[slot], head_size), state, head_size), head_size)


def finish_kernel(new_count, mine_ref, other_ref, out_ref):
    head_size = mine_ref.shape[0] - 8
    summed, _, total = merge(
        unpack(mine_ref[...], head_size), unpack(other_ref[...], head_size), head_size
    )
    rows = (summed / total).T.astype(out_ref.dtype)
    for head in range(rows.shape[0] // new_count):
        out_ref[:, head * head_size : (head + 1) * head_size] = rows[
            head * new_count : (head + 1) * new_count
        ]


def project_kernel(place_ref, rows_ref, weight_ref, out_ref):
    out_ref[...] = jnp.dot(rows_ref[...], weight_ref[...], preferred_element_type=F32)


def project_more_kernel(place_ref, rows_ref, weight_ref, before_ref, out_ref):
    out_ref[...] = before_ref[...] + jnp.dot(
        rows_ref[...], weight_ref[...], preferred_element_type=F32
    )


def project(place, rows, weight, tile=512):
    new_count, depth = rows.shape
    columns = weight.shape[1]
    return pl.pallas_call(
        project_kernel,
        out_shape=jax.ShapeDtypeStruct((new_count, columns), F32),
        grid_spec=pltpu.PrefetchScalarGridSpec(
            num_scalar_prefetch=1,
            grid=(columns // tile,),
            in_specs=[
                pl.BlockSpec((new_count, depth), lambda j, p: (0, 0)),
                pl.BlockSpec((depth, tile), lambda j, p: (p[0], j)),
            ],
            out_specs=pl.BlockSpec((new_count, tile), lambda j, p: (0, j)),
        ),
        compiler_params=params(),
        cost_estimate=pl.CostEstimate(
            flops=2 * new_count * depth * columns, bytes_accessed=2 * depth * columns, transcendentals=0
        ),
        name="project",
    )(place, rows, weight)


def project_more(place, rows, weight, before, own, tile=512):
    new_count, depth = rows.shape
    columns = weight.shape[1] // 2
    tiles = columns // tile

    def half(p):
        return p[1] if own else 1 - p[1]

    return pl.pallas_call(
        project_more_kernel,
        out_shape=jax.ShapeDtypeStruct((new_count, columns), F32),
        grid_spec=pltpu.PrefetchScalarGridSpec(
            num_scalar_prefetch=1,
            grid=(tiles,),
            in_specs=[
                pl.BlockSpec((new_count, depth), lambda j, p: (0, 0)),
                pl.BlockSpec((depth, tile), lambda j, p: (1 - p[0], half(p) * tiles + j)),
                pl.BlockSpec((new_count, tile), lambda j, p: (0, half(p) * tiles + j)),
            ],
            out_specs=pl.BlockSpec((new_count, tile), lambda j, p: (0, j)),
        ),
        compiler_params=params(),
        cost_estimate=pl.CostEstimate(
            flops=2 * new_count * depth * columns, bytes_accessed=2 * depth * columns, transcendentals=0
        ),
        name="project_own" if own else "project_sent",
    )(place, rows, weight, before)


def attend_cost(tokens, groups, lift, rows, head_size):
    flops = 2 * tokens * groups * (lift[0] * lift[1] + 2 * rows * head_size)
    return pl.CostEstimate(
        flops=flops, bytes_accessed=2 * tokens * lift[0], transcendentals=tokens * groups * rows
    )


def pair_shards(key_value_rows, queries, w_comp, latent_gain, w_up, w_out, replica_order):
    orders = list(itertools.permutations(range(lax.axis_size("rep"))))
    index = order_index(replica_order, orders)
    seq_at, tensor_at = lax.axis_index("seq"), lax.axis_index("tensor")
    core_at, chip_at = tensor_at % 2, tensor_at // 2
    place = jnp.stack([seq_at, core_at, chip_at]).astype(jnp.int32)
    _, new_count, heads, head_size = queries.shape
    groups = w_up.shape[0]
    rows = heads // groups * new_count

    query = jnp.swapaxes(queries[0], 0, 1).reshape(groups, rows, head_size)
    query = route(query, index, orders, False)

    tokens = key_value_rows.shape[1]
    latent = compress(key_value_rows[0].reshape(tokens, -1), w_comp, latent_gain)
    beside = swap(latent, "tensor", 1)
    across = swap(latent, "tensor", 2)
    across_beside = swap(across, "tensor", 1)

    state_shape = (head_size + 8, rows)
    first = pl.pallas_call(
        first_kernel,
        out_shape=jax.ShapeDtypeStruct((groups, *state_shape), F32),
        in_specs=[IN_SMEM] + [IN_VMEM] * 4,
        out_specs=IN_VMEM,
        compiler_params=params(),
        cost_estimate=attend_cost(2 * tokens, groups, w_up.shape[1:], rows, head_size),
        name="attend_chip",
    )(place, latent, beside, w_up, query)

    def later(slot):
        return pl.pallas_call(
            lambda *refs: later_kernel(slot, *refs),
            out_shape=jax.ShapeDtypeStruct(state_shape, F32),
            in_specs=[IN_SMEM] + [IN_VMEM] * 5,
            out_specs=IN_VMEM,
            compiler_params=params(),
            cost_estimate=attend_cost(2 * tokens, 1, w_up.shape[1:], rows, head_size),
            name="attend_own" if slot else "attend_sent",
        )(place, across, across_beside, w_up, query, first)

    other = swap(later(0), "seq", 1)
    mine = later(1)
    attended = pl.pallas_call(
        lambda *refs: finish_kernel(new_count, *refs),
        out_shape=jax.ShapeDtypeStruct((new_count, rows // new_count * head_size), BF16),
        in_specs=[IN_VMEM] * 2,
        out_specs=IN_VMEM,
        compiler_params=params(),
        name="finish",
    )(mine, other)

    attended = route(attended, index, orders, True)
    attended_other = swap(attended, "seq", 1)
    partial = project(place, attended, w_out)
    sent = swap(project_more(place, attended_other, w_out, partial, False), "tensor", 1)
    half = project_more(place, attended_other, w_out, partial, True) + sent
    quarter = half.shape[1] // 2
    low, high = half[:, :quarter], half[:, quarter:]
    upper = chip_at == 1
    arrived = swap(jnp.where(upper, low, high), "tensor", 2)
    summed = (jnp.where(upper, high, low) + arrived).astype(BF16)
    summed_across = swap(summed, "tensor", 2)
    half = jnp.where(
        upper,
        jnp.concatenate([summed_across, summed], axis=1),
        jnp.concatenate([summed, summed_across], axis=1),
    )
    half_beside = swap(half, "tensor", 1)
    whole = jnp.where(
        core_at == 1,
        jnp.concatenate([half_beside, half], axis=1),
        jnp.concatenate([half, half_beside], axis=1),
    )
    return whole[None]


def shards(key_value_rows, queries, w_comp, latent_gain, w_up, w_out, replica_order):
    orders = list(itertools.permutations(range(lax.axis_size("rep"))))
    index = order_index(replica_order, orders)
    query = route(queries[0], index, orders, False)
    rows = key_value_rows[0]
    latent = compress(rows.reshape(rows.shape[0], -1), w_comp, latent_gain)
    latent = lax.all_gather(latent, "tensor", axis=0, tiled=True)
    groups = w_up.shape[0]
    lifted = jnp.einsum("tf,gfy->tgy", latent, w_up, preferred_element_type=F32).astype(BF16)
    head_size = query.shape[-1]
    new_count = query.shape[0]
    keys = lifted[..., :head_size]
    values = lifted[..., head_size:]
    grouped_heads = query.reshape(new_count, groups, -1, head_size)
    scores = jnp.einsum(
        "nghd,tgd->nght", grouped_heads, keys, preferred_element_type=F32
    ) * head_size ** (-0.5)
    top = lax.pmax(jnp.max(scores, axis=-1), "seq")
    expo = jnp.exp(scores - top[..., None])
    total = jnp.sum(expo, axis=-1)
    summed = jnp.einsum("nght,tgd->nghd", expo.astype(BF16), values, preferred_element_type=F32)
    summed, total = lax.psum((summed, total), "seq")
    attended = (summed / total[..., None]).astype(BF16).reshape(new_count, -1)
    attended = route(attended, index, orders, True)
    partial = jnp.dot(attended, w_out, preferred_element_type=F32)
    return lax.psum(partial, "tensor").astype(BF16)[None]


def solution(mesh):
    placed = (
        P("rep", ("seq", "tensor"), None, None),
        P("rep", None, "tensor", None),
        P(),
        P(),
        P("tensor", None, None),
        P("tensor", "seq"),
        P(),
    )
    paired = mesh.shape["seq"] == 2 and mesh.shape["tensor"] == 4
    return jax.shard_map(
        pair_shards if paired else shards,
        mesh=mesh,
        in_specs=placed,
        out_specs=P("rep", None, "seq"),
        check_vma=False,
    )
```

time: 202 us -> 86.2 us (0.43)
  waiting for transfers between devices: 108 us -> 36.3 us
  blocking collectives: 37 us -> 0 us
  Pallas kernels: 0 us -> 24.4 us
  matrix products: 22.2 us -> 1.08 us
  starting transfers between devices: 4.46 us -> 18.4 us
  between operations: 13.2 us -> 0.73 us
  other arithmetic: 12.8 us -> 3.84 us
    all_gather x3 -> x0, waiting for transfers between devices: 87.3 us -> none  [the longest x1 43.4 us: shards(): piece = lax.all_gather(mixed, 'rep', axis=0, tiled=True)]
    ppermute x0 -> x11, waiting for transfers between devices: none -> 36.3 us  [the longest x9 25.5 us: swap(): return lax.ppermute(value, axis, pairs)]
    psum x2 -> x0, blocking collectives: 32 us -> none  [the longest x1 26.9 us: shards(): mixed = lax.psum(partial_output, 'tensor').astype(jnp.bfloat16)[None]]
    pallas_call x0 -> x7, Pallas kernels: none -> 24.4 us  [the longest x2 9.08 us: project_more(): pl.pallas_call(project_more_kernel, out_shape=jax.ShapeDtypeStruct((new_c...]
    dot_general x5 -> x1, matrix products: 22.2 us -> 1.08 us  [compress(): projected = jnp.dot(rows, weight, preferred_element_type=F32)]
    psum x1 -> x0, waiting for transfers between devices: 19.2 us -> none  [shards(): summed, total = lax.psum((summed, total), 'seq')]
    ppermute x0 -> x11, starting transfers between devices: none -> 18.4 us  [the longest x9 9.19 us: swap(): return lax.ppermute(value, axis, pairs)]
    reduce_sum x3 -> x1, other arithmetic: 7.54 us -> 0.6 us  [order_index(): return jnp.sum(jnp.where(match, lax.iota(jnp.int32, len(orders)), 0))]
  transfers between devices with their start and end apart: 5 -> 11, of which waited for: 4 -> 7; matrix products, arithmetic and copies ran while one was open for 8% -> 2% of each run, Pallas kernels for 0% -> 19%
where the time goes in v1:
time: 86.2 us; the launch traced here: 87.6 us
  waiting for transfers between devices  36.3 us (42%)
  Pallas kernels  24.4 us (28%)
  starting transfers between devices  18.4 us (21%)
  other arithmetic  3.84 us (4%)
  local copies, waits for them, and re-layouts  2.87 us (3%)
  matrix products  1.08 us (1%)
    ppermute x9, waiting for transfers between devices, swap(): return lax.ppermute(value, axis, pairs)  25.5 us
    ppermute x2, waiting for transfers between devices, branch(): return lambda v: lax.ppermute(v, 'rep', pairs)  10.7 us
    ppermute x9, starting transfers between devices, swap(): return lax.ppermute(value, axis, pairs)  9.19 us
    ppermute x2, starting transfers between devices, branch(): return lambda v: lax.ppermute(v, 'rep', pairs)  9.16 us
    pallas_call x2, Pallas kernels, project_more(): pl.pallas_call(project_more_kernel, out_shape=jax.ShapeDtypeStruct((new_c...  9.08 us
    pallas_call x1, Pallas kernels, project(): pl.pallas_call(project_kernel, out_shape=jax.ShapeDtypeStruct((new_count,...  7.35 us
    pallas_call x2, Pallas kernels, later(): pl.pallas_call(lambda *refs: later_kernel(slot, *refs), out_shape=jax.Sha...  4.45 us
    pallas_call x1, Pallas kernels, pair_shards(): pl.pallas_call(first_kernel, out_shape=jax.ShapeDtypeStruct((groups, *sta...  3.41 us
  transfers between devices with their start and end apart: 11, of which 7 were waited for; matrix products, arithmetic and copies ran while one was open for 2% of the time, Pallas kernels for 19%

profile of v1, /device:TPU:0, one launch (start us, length us, event | category | flops | bytes accessed | tf_op | source)
XLA Modules:
  0.0 87.6 jit_solution(6413730062155074455)
XLA Ops:
  0.0 0.0 copy-start
  0.0 2.0 %copy.11 = bf16[48,8,8,256]{3,1,2,0:T(8,128)(2,1)S(1)} copy(bf16[48,8,8,256]{3,2,1,0:T(8,128)(2,1)} %bitcast.14) | data formatting | bytes 3145728
  2.1 0.0 copy-done
  2.1 0.0 copy-start.2
  2.1 0.0 copy-start.3
  2.1 0.0 copy-start.5
  2.1 0.0 copy-start.1
  2.1 1.1 %multiply_reduce_fusion = (f32[384]{0:T(512)S(1)}, f32[384,512]{1,0:T(8,128)S(1)}) fusion(bf16[384,2048]{1,0:T(8,128)(2,1)S(1)} %bitcast.15, bf16[2048,512]{1,0:T(8,128)(2,1)S(1)} %copy-done), kind=kOutput, calls=%fused_computation.1 | convolution fusion | flops 805699200 | bytes 4457984 | tf_op jit(solution)/shard_map/dot_general | solution.py:22
  3.2 0.9 %multiply_convert_fusion.lat_a = bf16[384,512]{1,0:T(8,128)(2,1)} fusion(f32[384,512]{1,0:T(8,128)S(1)} %get-tuple-element.104, f32[512]{0:T(512)S(1)} %convert_element_type.9, f32[384]{0:T(512)S(1)} %add_rsqrt_fusion), kind=kLoop, calls=%fused_computation | loop fusion | flops 589824 | bytes 1183232 | tf_op jit(solution)/shard_map/convert_element_type | solution.py:24
  4.1 2.9 %collective-permute-start.48 = (bf16[384,512]{1,0:T(8,128)(2,1)}, bf16[384,512]{1,0:T(8,128)(2,1)S(1)}, u32[]{:S(2)}, u32[]{:S(2)}) collective-permute-start(bf16[384,512]{1,0:T(8,128)(2,1)} %multiply_convert_fusion.lat_a), channel_id=1, source_target_pairs={{0,2},{1,3},{2,0},{3,1},{4,6},{5,7},{6,4},{7,5},{8,10},{9,11},{10,... | collective-permute-start | bytes 1179656 | tf_op jit(solution)/shard_map/ppermute | solution.py:43
  7.1 0.0 collective-permute-start.50
  7.1 0.8 copy.10
  7.9 8.5 %collective-permute-done.48.refs_1_ = bf16[384,512]{1,0:T(8,128)(2,1)S(1)} collective-permute-done((bf16[384,512]{1,0:T(8,128)(2,1)}, bf16[384,512]{1,0:T(8,128)(2,1)S(1)}, u32[]{:S(2)}, u32[]{:S(2)}) %collective-permute-start.48) | collective-permute-done | bytes 393248 | tf_op jit(solution)/shard_map/ppermute | solution.py:43
  16.4 0.0 collective-permute-start.49
  16.4 0.1 compare_reduce_fusion
  16.5 0.6 select_reduce_fusion
  17.6 12.1 %conditional.2 = (bf16[2,512,128]{2,1,0:T(8,128)(2,1)}) conditional(s32[]{:T(128)} %clamp.4, bf16[2,512,128]{2,1,0:T(8,128)(2,1)} %bitcast.29, bf16[2,512,128]{2,1,0:T(8,128)(2,1)} %bitcast.19, bf16[2,512,128]{2,1,0:T(8,128)(2,1)} %bitcast.20, bf16[2,512,128]{2,1,0:T(8,128)(2,1)} %bitcast.21, ...), branch_computations={%region_3.4_spmd, %region_4.5_spmd, %region_5.6_spmd, %region_6.7_... | conditional | bytes 1048624 | solution.py:38
  17.7 4.8 %collective-permute-start.14 = (bf16[2,512,128]{2,1,0:T(8,128)(2,1)}, bf16[2,512,128]{2,1,0:T(8,128)(2,1)}, u32[]{:S(2)}, u32[]{:S(2)}) collective-permute-start(bf16[2,512,128]{2,1,0:T(8,128)(2,1)} %param.14), channel_id=1, source_target_pairs={{0,8},{4,4},{8,0},{12,12},{1,9},{5,5},{9,1},{13,13},{2,10},{6,6},{... | collective-permute-start | bytes 786440 | tf_op jit(solution)/shard_map/cond/branch_14_fun/ppermute | solution.py:36
  22.4 7.3 %collective-permute-done.14 = bf16[2,512,128]{2,1,0:T(8,128)(2,1)} collective-permute-done((bf16[2,512,128]{2,1,0:T(8,128)(2,1)}, bf16[2,512,128]{2,1,0:T(8,128)(2,1)}, u32[]{:S(2)}, u32[]{:S(2)}) %collective-permute-start.14) | collective-permute-done | bytes 262176 | tf_op jit(solution)/shard_map/cond/branch_14_fun/ppermute | solution.py:36
  29.7 0.1 pad_add_fusion.place_ref.refs_0_
  29.8 0.0 collective-permute-done.50.lat_b
  29.8 0.0 copy-done.1
  29.8 3.4 %attend_chip.1.refs_5_ = f32[2,136,512]{2,1,0:T(8,128)S(1)} custom-call(s32[3]{0:T(128)S(1)} %pad_add_fusion.place_ref.refs_0_, bf16[384,512]{1,0:T(8,128)(2,1)} %multiply_convert_fusion.lat_a, bf16[384,512]{1,0:T(8,128)(2,1)} %collective-permute-done.50.lat_b, bf16[2,512,256]{2,1,0:T(8,128)(2,1)S(1)} %copy-done.1, ...), custom_call_target="tpu_custom_call" | custom-call | flops 805306368 | bytes 786432 | tf_op jit(solution)/shard_map/attend_chip/pallas_call | solution.py:211
  33.2 0.0 collective-permute-done.49.refs_2_
  33.2 2.2 %attend_sent.1 = f32[136,512]{1,0:T(8,128)S(1)} custom-call(s32[3]{0:T(128)S(1)} %pad_add_fusion.place_ref.refs_0_, bf16[384,512]{1,0:T(8,128)(2,1)S(1)} %collective-permute-done.48.refs_1_, bf16[384,512]{1,0:T(8,128)(2,1)S(1)} %collective-permute-done.49.refs_2_, bf16[2,512,256]{2,1,0:T(8,128)(2,1)S(1)} %copy-done.1, ...), custom_call_target="tpu_custom_call" | custom-call | flops 402653184 | bytes 786432 | tf_op jit(solution)/shard_map/attend_sent/pallas_call | solution.py:222
  35.4 1.6 %collective-permute-start.51 = (f32[136,512]{1,0:T(8,128)S(1)}, f32[136,512]{1,0:T(8,128)S(1)}, u32[]{:S(2)}, u32[]{:S(2)}) collective-permute-start(f32[136,512]{1,0:T(8,128)S(1)} %attend_sent.1), channel_id=1, source_target_pairs={{0,16},{16,0},{1,17},{17,1},{2,18},{18,2},{3,19},{19,3},{4,20},{20... | collective-permute-start | bytes 835592 | tf_op jit(solution)/shard_map/ppermute | solution.py:43
  37.1 2.2 %attend_own.1.refs_0_ = f32[136,512]{1,0:T(8,128)S(1)} custom-call(s32[3]{0:T(128)S(1)} %pad_add_fusion.place_ref.refs_0_, bf16[384,512]{1,0:T(8,128)(2,1)S(1)} %collective-permute-done.48.refs_1_, bf16[384,512]{1,0:T(8,128)(2,1)S(1)} %collective-permute-done.49.refs_2_, bf16[2,512,256]{2,1,0:T(8,128)(2,1)S(1)} %copy-done.1, ...), custom_call_target="tpu_custom_call" | custom-call | flops 402653184 | bytes 786432 | tf_op jit(solution)/shard_map/attend_own/pallas_call | solution.py:222
  39.3 4.6 %collective-permute-done.51.refs_1_ = f32[136,512]{1,0:T(8,128)S(1)} collective-permute-done((f32[136,512]{1,0:T(8,128)S(1)}, f32[136,512]{1,0:T(8,128)S(1)}, u32[]{:S(2)}, u32[]{:S(2)}) %collective-permute-start.51) | collective-permute-done | bytes 278560 | tf_op jit(solution)/shard_map/ppermute | solution.py:43
  43.9 0.1 finish.1
  44.1 7.9 %conditional.3 = (bf16[64,1024]{1,0:T(8,128)(2,1)}) conditional(s32[]{:T(128)} %clamp.4, bf16[64,1024]{1,0:T(8,128)(2,1)S(1)} %finish.1, bf16[64,1024]{1,0:T(8,128)(2,1)S(1)} %finish.1, bf16[64,1024]{1,0:T(8,128)(2,1)S(1)} %finish.1, bf16[64,1024]{1,0:T(8,128)(2,1)S(1)} %finish.1, ...), branch_computations={%region_27.28_spmd, %region_28.29_spmd, %region_29.30_spmd, %regio... | conditional | bytes 524336 | solution.py:38
  44.1 4.4 %collective-permute-start.38 = (bf16[64,1024]{1,0:T(8,128)(2,1)S(1)}, bf16[64,1024]{1,0:T(8,128)(2,1)}, u32[]{:S(2)}, u32[]{:S(2)}) collective-permute-start(bf16[64,1024]{1,0:T(8,128)(2,1)S(1)} %param.38), channel_id=1, source_target_pairs={{8,0},{4,4},{0,8},{12,12},{9,1},{5,5},{1,9},{13,13},{10,2},{6,6},{... | collective-permute-start | bytes 393224 | tf_op jit(solution)/shard_map/cond/branch_14_fun/ppermute | solution.py:36
  48.5 3.4 %collective-permute-done.38 = bf16[64,1024]{1,0:T(8,128)(2,1)} collective-permute-done((bf16[64,1024]{1,0:T(8,128)(2,1)S(1)}, bf16[64,1024]{1,0:T(8,128)(2,1)}, u32[]{:S(2)}, u32[]{:S(2)}) %collective-permute-start.38) | collective-permute-done | bytes 131104 | tf_op jit(solution)/shard_map/cond/branch_14_fun/ppermute | solution.py:36
  52.0 1.4 %collective-permute-start.52 = (bf16[64,1024]{1,0:T(8,128)(2,1)}, bf16[64,1024]{1,0:T(8,128)(2,1)S(1)}, u32[]{:S(2)}, u32[]{:S(2)}) collective-permute-start(bf16[64,1024]{1,0:T(8,128)(2,1)} %get-tuple-element.106.rows_ref), channel_id=1, source_target_pairs={{0,16},{16,0},{1,17},{17,1},{2,18},{18,2},{3,19},{19,3},{4,20},{20... | collective-permute-start | bytes 393224 | tf_op jit(solution)/shard_map/ppermute | solution.py:43
  53.4 7.3 %project.1.before_ref = f32[64,4096]{1,0:T(8,128)S(1)} custom-call(s32[3]{0:T(128)S(1)} %pad_add_fusion.place_ref.refs_0_, bf16[64,1024]{1,0:T(8,128)(2,1)} %get-tuple-element.106.rows_ref, bf16[2048,4096]{1,0:T(8,128)(2,1)} %weight_ref.5), custom_call_target="tpu_custom_call" | custom-call | flops 536870912 | bytes 8388608 | tf_op jit(solution)/shard_map/project/pallas_call | solution.py:135
  60.8 0.0 collective-permute-done.52.rows_ref
  60.8 5.0 %project_sent.1 = f32[64,2048]{1,0:T(8,128)} custom-call(s32[3]{0:T(128)S(1)} %pad_add_fusion.place_ref.refs_0_, bf16[64,1024]{1,0:T(8,128)(2,1)S(1)} %collective-permute-done.52.rows_ref, bf16[2048,4096]{1,0:T(8,128)(2,1)} %weight_ref.5, f32[64,4096]{1,0:T(8,128)S(1)} %project.1.before_ref), custom_call_target="tpu_custom_call" | custom-call | flops 268435456 | bytes 4194304 | tf_op jit(solution)/shard_map/project_sent/pallas_call | solution.py:163
  65.8 0.0 collective-permute-start.53
  65.8 4.1 %project_own.1 = f32[64,2048]{1,0:T(8,128)S(1)} custom-call(s32[3]{0:T(128)S(1)} %pad_add_fusion.place_ref.refs_0_, bf16[64,1024]{1,0:T(8,128)(2,1)S(1)} %collective-permute-done.52.rows_ref, bf16[2048,4096]{1,0:T(8,128)(2,1)} %weight_ref.5, f32[64,4096]{1,0:T(8,128)S(1)} %project.1.before_ref), custom_call_target="tpu_custom_call" | custom-call | flops 268435456 | bytes 4194304 | tf_op jit(solution)/shard_map/project_own/pallas_call | solution.py:163
  69.9 0.0 collective-permute-done.53
  69.9 1.1 %add.25 = f32[64,2048]{1,0:T(8,128)S(1)} add(f32[64,2048]{1,0:T(8,128)S(1)} %project_own.1, f32[64,2048]{1,0:T(8,128)} %collective-permute-done.53) | non-fusion elementwise | flops 131072 | bytes 1572864 | tf_op jit(solution)/shard_map/add | solution.py:247
  71.0 1.6 %collective-permute-start.54 = (f32[64,1024]{1,0:T(8,128)S(1)}, f32[64,1024]{1,0:T(8,128)S(1)}, u32[]{:S(2)}, u32[]{:S(2)}) collective-permute-start(f32[64,1024]{1,0:T(8,128)S(1)} %slice_select_fusion), channel_id=1, source_target_pairs={{0,2},{1,3},{2,0},{3,1},{4,6},{5,7},{6,4},{7,5},{8,10},{9,11},{10,... | collective-permute-start | bytes 786440 | tf_op jit(solution)/shard_map/ppermute | solution.py:43
  72.6 7.2 %collective-permute-done.54 = f32[64,1024]{1,0:T(8,128)S(1)} collective-permute-done((f32[64,1024]{1,0:T(8,128)S(1)}, f32[64,1024]{1,0:T(8,128)S(1)}, u32[]{:S(2)}, u32[]{:S(2)}) %collective-permute-start.54) | collective-permute-done | bytes 262176 | tf_op jit(solution)/shard_map/ppermute | solution.py:43
  79.8 1.6 %collective-permute-start.55 = (bf16[64,1024]{1,0:T(8,128)(2,1)S(1)}, bf16[64,1024]{1,0:T(8,128)(2,1)S(1)}, u32[]{:S(2)}, u32[]{:S(2)}) collective-permute-start(bf16[64,1024]{1,0:T(8,128)(2,1)S(1)} %add_convert_fusion), channel_id=1, source_target_pairs={{0,2},{1,3},{2,0},{3,1},{4,6},{5,7},{6,4},{7,5},{8,10},{9,11},{10,... | collective-permute-start | bytes 393224 | tf_op jit(solution)/shard_map/ppermute | solution.py:43
  81.4 3.6 %collective-permute-done.55 = bf16[64,1024]{1,0:T(8,128)(2,1)S(1)} collective-permute-done((bf16[64,1024]{1,0:T(8,128)(2,1)S(1)}, bf16[64,1024]{1,0:T(8,128)(2,1)S(1)}, u32[]{:S(2)}, u32[]{:S(2)}) %collective-permute-start.55) | collective-permute-done | bytes 131104 | tf_op jit(solution)/shard_map/ppermute | solution.py:43
  85.0 0.1 maximum_select_fusion.1
  85.1 0.1 collective-permute-start.56
  85.2 1.5 %collective-permute-done.56 = bf16[64,2048]{1,0:T(8,128)(2,1)S(1)} collective-permute-done((bf16[64,2048]{1,0:T(8,128)(2,1)S(1)}, bf16[64,2048]{1,0:T(8,128)(2,1)S(1)}, u32[]{:S(2)}, u32[]{:S(2)}) %collective-permute-start.56) | collective-permute-done | bytes 262176 | tf_op jit(solution)/shard_map/ppermute | solution.py:43
  86.7 0.9 %maximum_select_fusion = bf16[1,64,4096]{2,1,0:T(8,128)(2,1)} fusion(bf16[1,64,2048]{2,1,0:T(8,128)(2,1)S(1)} %bitcast.16, bf16[1,64,2048]{2,1,0:T(8,128)(2,1)S(1)} %bitcast.42, pred[]{:T(512)S(6)} %eq.16), kind=kLoop, calls=%fused_computation.2 | loop fusion | flops 2359296 | bytes 1048577 | tf_op jit(solution)/shard_map/jit(_where)/select_n | solution.py:260
  (9 shorter events, 0.1 us)
Async XLA Ops:
  0.0 2.1 %copy-start = (bf16[2048,512]{1,0:T(8,128)(2,1)S(1)}, bf16[2048,512]{1,0:T(8,128)(2,1)}, u32[]{:S(2)}) copy-start(bf16[2048,512]{1,0:T(8,128)(2,1)} %param.58) | copy-start | bytes 6291460
  2.1 1.2 %copy-start.4 = (bf16[512]{0:T(512)(128)(2,1)S(1)}, bf16[512]{0:T(512)(128)(2,1)}, u32[]{:S(2)}) copy-start(bf16[512]{0:T(512)(128)(2,1)} %param.59) | copy-start | bytes 3076
  2.1 5.0 %copy-start.2 = (bf16[1,64,16,128]{3,2,1,0:T(8,128)(2,1)S(1)}, bf16[1,64,16,128]{3,2,1,0:T(8,128)(2,1)}, u32[]{:S(2)}) copy-start(bf16[1,64,16,128]{3,2,1,0:T(8,128)(2,1)} %param.57) | copy-start | bytes 786436
  2.1 14.3 %copy-start.3 = (s32[24,4]{0,1:T(4,128)S(1)}, s32[24,4]{0,1:T(4,128)}, u32[]{:S(2)}) copy-start(s32[24,4]{0,1:T(4,128)} %constant.49.clone) | copy-start | bytes 1156
  2.1 14.3 %copy-start.5 = (s32[4]{0:T(128)S(1)}, s32[4]{0:T(128)}, u32[]{:S(2)}) copy-start(s32[4]{0:T(128)} %param.62) | copy-start | bytes 52
  2.1 27.7 %copy-start.1 = (bf16[2,512,256]{2,1,0:T(8,128)(2,1)S(1)}, bf16[2,512,256]{2,1,0:T(8,128)(2,1)}, u32[]{:S(2)}) copy-start(bf16[2,512,256]{2,1,0:T(8,128)(2,1)} %refs_3_.3) | copy-start | bytes 1572868
  4.1 12.3 %collective-permute-start.48 = (bf16[384,512]{1,0:T(8,128)(2,1)}, bf16[384,512]{1,0:T(8,128)(2,1)S(1)}, u32[]{:S(2)}, u32[]{:S(2)}) collective-permute-start(bf16[384,512]{1,0:T(8,128)(2,1)} %multiply_convert_fusion.lat_a), channel_id=1, source_target_pairs={{0,2},{1,3},{2,0},{3,1},{4,6},{5,7},{6,4},{7,5},{8,10},{9,11},{10,... | collective-permute-start | bytes 1179656 | tf_op jit(solution)/shard_map/ppermute | solution.py:43
  7.1 22.7 %collective-permute-start.50 = (bf16[384,512]{1,0:T(8,128)(2,1)}, bf16[384,512]{1,0:T(8,128)(2,1)}, u32[]{:S(2)}, u32[]{:S(2)}) collective-permute-start(bf16[384,512]{1,0:T(8,128)(2,1)} %multiply_convert_fusion.lat_a), channel_id=1, source_target_pairs={{0,1},{1,0},{2,3},{3,2},{4,5},{5,4},{6,7},{7,6},{8,9},{9,8},{10,11... | collective-permute-start | bytes 1179656 | tf_op jit(solution)/shard_map/ppermute | solution.py:43
  16.4 16.8 %collective-permute-start.49 = (bf16[384,512]{1,0:T(8,128)(2,1)S(1)}, bf16[384,512]{1,0:T(8,128)(2,1)S(1)}, u32[]{:S(2)}, u32[]{:S(2)}) collective-permute-start(bf16[384,512]{1,0:T(8,128)(2,1)S(1)} %collective-permute-done.48.refs_1_), channel_id=1, source_target_pairs={{0,1},{1,0},{2,3},{3,2},{4,5},{5,4},{6,7},{7,6},{8,9},{9,8},{10,11... | collective-permute-start | bytes 1179656 | tf_op jit(solution)/shard_map/ppermute | solution.py:43
  17.7 12.0 %collective-permute-start.14 = (bf16[2,512,128]{2,1,0:T(8,128)(2,1)}, bf16[2,512,128]{2,1,0:T(8,128)(2,1)}, u32[]{:S(2)}, u32[]{:S(2)}) collective-permute-start(bf16[2,512,128]{2,1,0:T(8,128)(2,1)} %param.14), channel_id=1, source_target_pairs={{0,8},{4,4},{8,0},{12,12},{1,9},{5,5},{9,1},{13,13},{2,10},{6,6},{... | collective-permute-start | bytes 786440 | tf_op jit(solution)/shard_map/cond/branch_14_fun/ppermute | solution.py:36
  35.4 8.5 %collective-permute-start.51 = (f32[136,512]{1,0:T(8,128)S(1)}, f32[136,512]{1,0:T(8,128)S(1)}, u32[]{:S(2)}, u32[]{:S(2)}) collective-permute-start(f32[136,512]{1,0:T(8,128)S(1)} %attend_sent.1), channel_id=1, source_target_pairs={{0,16},{16,0},{1,17},{17,1},{2,18},{18,2},{3,19},{19,3},{4,20},{20... | collective-permute-start | bytes 835592 | tf_op jit(solution)/shard_map/ppermute | solution.py:43
  44.1 7.9 %collective-permute-start.38 = (bf16[64,1024]{1,0:T(8,128)(2,1)S(1)}, bf16[64,1024]{1,0:T(8,128)(2,1)}, u32[]{:S(2)}, u32[]{:S(2)}) collective-permute-start(bf16[64,1024]{1,0:T(8,128)(2,1)S(1)} %param.38), channel_id=1, source_target_pairs={{8,0},{4,4},{0,8},{12,12},{9,1},{5,5},{1,9},{13,13},{10,2},{6,6},{... | collective-permute-start | bytes 393224 | tf_op jit(solution)/shard_map/cond/branch_14_fun/ppermute | solution.py:36
  52.0 8.8 %collective-permute-start.52 = (bf16[64,1024]{1,0:T(8,128)(2,1)}, bf16[64,1024]{1,0:T(8,128)(2,1)S(1)}, u32[]{:S(2)}, u32[]{:S(2)}) collective-permute-start(bf16[64,1024]{1,0:T(8,128)(2,1)} %get-tuple-element.106.rows_ref), channel_id=1, source_target_pairs={{0,16},{16,0},{1,17},{17,1},{2,18},{18,2},{3,19},{19,3},{4,20},{20... | collective-permute-start | bytes 393224 | tf_op jit(solution)/shard_map/ppermute | solution.py:43
  65.8 4.1 %collective-permute-start.53 = (f32[64,2048]{1,0:T(8,128)}, f32[64,2048]{1,0:T(8,128)}, u32[]{:S(2)}, u32[]{:S(2)}) collective-permute-start(f32[64,2048]{1,0:T(8,128)} %project_sent.1), channel_id=1, source_target_pairs={{0,1},{1,0},{2,3},{3,2},{4,5},{5,4},{6,7},{7,6},{8,9},{9,8},{10,11... | collective-permute-start | bytes 1572872 | tf_op jit(solution)/shard_map/ppermute | solution.py:43
  71.0 8.8 %collective-permute-start.54 = (f32[64,1024]{1,0:T(8,128)S(1)}, f32[64,1024]{1,0:T(8,128)S(1)}, u32[]{:S(2)}, u32[]{:S(2)}) collective-permute-start(f32[64,1024]{1,0:T(8,128)S(1)} %slice_select_fusion), channel_id=1, source_target_pairs={{0,2},{1,3},{2,0},{3,1},{4,6},{5,7},{6,4},{7,5},{8,10},{9,11},{10,... | collective-permute-start | bytes 786440 | tf_op jit(solution)/shard_map/ppermute | solution.py:43
  79.8 5.2 %collective-permute-start.55 = (bf16[64,1024]{1,0:T(8,128)(2,1)S(1)}, bf16[64,1024]{1,0:T(8,128)(2,1)S(1)}, u32[]{:S(2)}, u32[]{:S(2)}) collective-permute-start(bf16[64,1024]{1,0:T(8,128)(2,1)S(1)} %add_convert_fusion), channel_id=1, source_target_pairs={{0,2},{1,3},{2,0},{3,1},{4,6},{5,7},{6,4},{7,5},{8,10},{9,11},{10,... | collective-permute-start | bytes 393224 | tf_op jit(solution)/shard_map/ppermute | solution.py:43
  85.1 1.6 %collective-permute-start.56 = (bf16[64,2048]{1,0:T(8,128)(2,1)S(1)}, bf16[64,2048]{1,0:T(8,128)(2,1)S(1)}, u32[]{:S(2)}, u32[]{:S(2)}) collective-permute-start(bf16[64,2048]{1,0:T(8,128)(2,1)S(1)} %maximum_select_fusion.1), channel_id=1, source_target_pairs={{0,1},{1,0},{2,3},{3,2},{4,5},{5,4},{6,7},{7,6},{8,9},{9,8},{10,11... | collective-permute-start | bytes 786440 | tf_op jit(solution)/shard_map/ppermute | solution.py:43

commit v2 on v0

v2 whole, which is shorter than its diff:
```python
import itertools
import math

import jax
import jax.numpy as jnp
from jax import lax
from jax.experimental import pallas as pl
from jax.experimental.pallas import tpu as pltpu
from jax.sharding import PartitionSpec as P

BF16, F32 = jnp.bfloat16, jnp.float32
MIB = 1024 * 1024
IN_VMEM = pl.BlockSpec(memory_space=pltpu.VMEM)
IN_SMEM = pl.BlockSpec(memory_space=pltpu.SMEM)
ANYWHERE = pl.BlockSpec(memory_space=pl.ANY)
COPIES = 8


def shape(dims, dtype):
    return jax.ShapeDtypeStruct(dims, dtype)


def call(body, name, outs, operands, vmem, scratch=(), smem_in=0, smem_out=False, any_in=0, cost=None):
    specs = [IN_SMEM] * smem_in + [IN_VMEM] * (len(operands) - smem_in - any_in) + [ANYWHERE] * any_in
    out_specs = [IN_VMEM] * len(outs)
    if smem_out:
        out_specs[-1] = IN_SMEM
    return pl.pallas_call(
        body,
        out_shape=outs,
        in_specs=specs,
        out_specs=out_specs,
        scratch_shapes=list(scratch),
        compiler_params=pltpu.CompilerParams(vmem_limit_bytes=vmem * MIB),
        cost_estimate=cost,
        name=name,
    )(*operands)


def cost(flops, moved, exps=0):
    return pl.CostEstimate(flops=int(flops), bytes_accessed=int(moved), transcendentals=int(exps))


def dot(a, b):
    return jnp.dot(a, b, preferred_element_type=F32)


def compress(rows, weight, gain):
    projected = dot(rows, weight)
    scale = lax.rsqrt(jnp.mean(projected * projected, axis=-1, keepdims=True) + 1e-06)
    return (projected * scale * gain.astype(F32)[None]).astype(BF16)


def order_index(replica_order, orders):
    table = jnp.array(orders, jnp.int32)
    match = jnp.all(table == replica_order[None], axis=1)
    return jnp.sum(jnp.where(match, lax.iota(jnp.int32, len(orders)), 0))


def route_pairs(order, back):
    return [(p, r) if back else (r, p) for r, p in enumerate(order)]


def route(value, index, orders, back):
    def branch(order):
        return lambda v: lax.ppermute(v, "rep", route_pairs(order, back))

    return lax.switch(index, [branch(o) for o in orders], value)


def swap(value, axis, bit):
    pairs = [(i, i ^ bit) for i in range(lax.axis_size(axis))]
    return lax.ppermute(value, axis, pairs)


def cross(value, seq_core):
    pairs = [(i, i ^ (4 if i % 2 == seq_core else 2)) for i in range(8)]
    return lax.ppermute(value, ("seq", "tensor"), pairs)


def compress_kernel(order_ref, rows_ref, weight_ref, gain_ref, query_ref, latent_ref, half_ref, index_ref, wide):
    tokens, groups, width = rows_ref.shape
    lanes = wide.shape[2]
    for part in range(wide.shape[0]):
        values = rows_ref[:, :, part * lanes : (part + 1) * lanes].astype(F32)
        wide[part] = values.reshape(tokens * groups, lanes)
    projected = jnp.zeros((tokens, weight_ref.shape[1]), F32)
    for group in range(groups):
        picked = [
            wide[part, pl.ds(group, tokens, stride=groups), :] for part in range(wide.shape[0])
        ]
        picked = jnp.concatenate(picked, axis=1).astype(BF16)
        projected += dot(picked, weight_ref[group * width : (group + 1) * width, :])
    scale = lax.rsqrt(jnp.mean(projected * projected, axis=-1, keepdims=True) + 1e-06)
    latent_ref[...] = (projected * scale * gain_ref[...].astype(F32)).astype(BF16)

    new_count, heads, head_size = query_ref.shape
    query = query_ref[...].astype(F32)
    upper = lax.axis_index("seq") == 1
    query = jnp.where(upper, query[:, heads // 2 :], query[:, : heads // 2])
    half_ref[...] = query.reshape(half_ref.shape).astype(BF16)

    count = order_ref.shape[0]
    index = 0
    for i in range(count):
        smaller = 0
        for j in range(i + 1, count):
            smaller = smaller + (order_ref[j] < order_ref[i]).astype(jnp.int32)
        index = index + smaller * math.factorial(count - 1 - i)
    index_ref[0] = index


def score_kernel(parts, *refs):
    latent_refs, (lift_ref, query_ref), (score_ref, value_ref, top_ref) = (
        refs[:parts],
        refs[parts : parts + 2],
        refs[parts + 2 :],
    )
    head_size = query_ref.shape[-1]
    lift = lift_ref[lax.axis_index("seq")]
    query = query_ref[...]
    top = None
    for part, latent_ref in enumerate(latent_refs):
        tokens = latent_ref.shape[0]
        at = slice(part * tokens, (part + 1) * tokens)
        lifted = dot(latent_ref[...], lift).astype(BF16)
        score = lax.dot_general(
            lifted[:, :head_size], query, (((1,), (1,)), ((), ())), preferred_element_type=F32
        )
        score_ref[at] = score
        value_ref[at] = lifted[:, head_size:]
        part_top = jnp.max(score, axis=0, keepdims=True)
        top = part_top if top is None else jnp.maximum(top, part_top)
    top_ref[...] = jnp.broadcast_to(top, top_ref.shape)


def score_and_fetch_kernel(parts, *refs):
    *refs, held_ref, sems = refs
    weight_ref = refs.pop(parts + 2)
    rows = weight_ref.shape[0] // COPIES
    copies = []
    for i in range(COPIES):
        at = pl.ds(i * rows, rows)
        copies.append(pltpu.make_async_copy(weight_ref.at[at], held_ref.at[at], sems.at[i]))
    for copy in copies:
        copy.start()
    score_kernel(parts, *refs)
    for copy in copies:
        copy.wait()


def score_call(name, latents, lift, query, weight=None):
    tokens = sum(latent.shape[0] for latent in latents)
    rows, head_size = query.shape
    flops = 2 * tokens * (lift.shape[1] * lift.shape[2] + rows * head_size)
    outs = [shape((tokens, rows), F32), shape((tokens, head_size), BF16), shape((8, rows), F32)]
    operands = [*latents, lift, query]
    estimate = cost(flops, 6 * tokens * rows)
    if weight is None:
        body = lambda *refs: score_kernel(len(latents), *refs)
        return call(body, name, outs, operands, 16, cost=estimate)
    return call(
        lambda *refs: score_and_fetch_kernel(len(latents), *refs),
        name,
        [*outs, pltpu.VMEM(weight.shape, weight.dtype)],
        [*operands, weight],
        12,
        scratch=[pltpu.SemaphoreType.DMA((COPIES,))],
        any_in=1,
        cost=cost(flops, 2 * weight.shape[0] * weight.shape[1]),
    )


def attend_kernel(new_count, block, *refs):
    (*score_refs, out_ref, turned) = refs
    triples = [score_refs[i : i + 3] for i in range(0, len(score_refs), 3)]
    head_size = triples[0][1].shape[-1]
    coef = head_size ** (-0.5) * math.log2(math.e)
    top = triples[0][2][:1]
    for triple in triples[1:]:
        top = jnp.maximum(top, triple[2][:1])
    total = jnp.zeros_like(top)
    summed = jnp.zeros((head_size, top.shape[1]), F32)
    for score_ref, value_ref, _ in triples:
        for start in range(0, score_ref.shape[0], block):
            at = slice(start, start + block)
            expo = jnp.exp2((score_ref[at] - top) * coef)
            total += jnp.sum(expo, axis=0, keepdims=True)
            summed += lax.dot_general(
                value_ref[at], expo.astype(BF16), (((0,), (0,)), ((), ())), preferred_element_type=F32
            )
    turned[...] = (summed / total).T
    heads = turned.shape[0] // new_count
    for head in range(heads):
        out_ref[:, head * head_size : (head + 1) * head_size] = turned[
            pl.ds(head, new_count, stride=heads), :
        ].astype(BF16)


def project_kernel(tile, rows_ref, weight_ref, out_ref):
    depth = rows_ref.shape[1]
    start = pl.multiple_of(lax.axis_index("seq") * depth, depth)
    rows = rows_ref[...]
    width = out_ref.shape[2]
    for part in range(out_ref.shape[0]):
        for column in range(0, width, tile):
            at = part * width + column
            out_ref[part, :, column : column + tile] = dot(
                rows, weight_ref[pl.ds(start, depth), at : at + tile]
            )


def project_more_kernel(tile, own, rows_ref, weight_ref, before_ref, *refs):
    out_ref = refs[-1]
    depth = rows_ref.shape[1]
    start = pl.multiple_of((1 - lax.axis_index("seq")) * depth, depth)
    core = lax.axis_index("tensor") % 2
    part = core if own else 1 - core
    rows = rows_ref[...]
    width = out_ref.shape[1]
    for column in range(0, width, tile):
        at = pl.multiple_of(part * width + column, tile)
        value = before_ref[part, :, column : column + tile] + dot(
            rows, weight_ref[pl.ds(start, depth), pl.ds(at, tile)]
        )
        out_ref[:, column : column + tile] = value


def square_shards(key_value_rows, queries, w_comp, latent_gain, w_up, w_out, replica_order):
    orders = list(itertools.permutations(range(lax.axis_size("rep"))))
    tensor_at = lax.axis_index("tensor")
    core_at, chip_at = tensor_at % 2, tensor_at // 2
    _, new_count, heads, head_size = queries.shape
    _, tokens, all_groups, width = key_value_rows.shape
    latent_width = w_comp.shape[1]
    rows = heads // 2 * new_count

    latent, query, index = call(
        compress_kernel,
        "compress",
        [shape((tokens, latent_width), BF16), shape((rows, head_size), BF16), shape((1,), jnp.int32)],
        [replica_order, key_value_rows[0], w_comp, latent_gain[None], queries[0]],
        16,
        scratch=[pltpu.VMEM((width // 128, tokens * all_groups, 128), F32)],
        smem_in=1,
        smem_out=True,
        cost=cost(2 * tokens * all_groups * width * latent_width, 2 * tokens * all_groups * width),
    )

    def branch(order):
        def run(latent, query):
            return (
                cross(latent, 0),
                cross(latent, 1),
                swap(latent, "tensor", 1),
                lax.ppermute(query, "rep", route_pairs(order, False)),
            )

        return run

    near, far, beside, query = lax.switch(index[0], [branch(o) for o in orders], latent, query)
    corner = cross(near, 1)
    near_beside = swap(near, "tensor", 1)
    far_beside = swap(far, "tensor", 1)
    corner_beside = swap(corner, "tensor", 1)
    *first, held = score_call("score_chip", [latent, beside], w_up, query, w_out)
    second = score_call("score_next", [near, near_beside, far, far_beside], w_up, query)
    third = score_call("score_corner", [corner, corner_beside], w_up, query)
    depth = rows // new_count * head_size
    (attended,) = call(
        lambda *refs: attend_kernel(new_count, tokens, *refs),
        "attend",
        [shape((new_count, depth), BF16)],
        [*first, *second, *third],
        16,
        scratch=[pltpu.VMEM((rows, head_size), F32)],
        cost=cost(2 * 8 * tokens * rows * head_size, 8 * tokens * rows * 4, 8 * tokens * rows),
    )

    attended = route(attended, index[0], orders, True)
    attended_other = swap(attended, "seq", 1)
    columns = w_out.shape[1]
    tile = min(512, columns // 2)
    (partial,) = call(
        lambda *refs: project_kernel(tile, *refs),
        "project",
        [shape((2, new_count, columns // 2), F32)],
        [attended, held],
        12,
        cost=cost(2 * new_count * depth * columns, 2 * depth * columns),
    )

    def project_more(own, name):
        return call(
            lambda *refs: project_more_kernel(tile, own, *refs),
            name,
            [shape((new_count, columns // 2), F32)],
            [attended_other, held, partial],
            12,
            cost=cost(new_count * depth * columns, depth * columns),
        )[0]

    sent = swap(project_more(False, "project_sent"), "tensor", 1)
    half = project_more(True, "project_own") + sent
    quarter = half.shape[1] // 2
    low, high = half[:, :quarter], half[:, quarter:]
    upper = chip_at == 1
    arrived = swap(jnp.where(upper, low, high), "tensor", 2)
    summed = (jnp.where(upper, high, low) + arrived).astype(BF16)
    summed_across = swap(summed, "tensor", 2)
    half = jnp.where(
        upper,
        jnp.concatenate([summed_across, summed], axis=1),
        jnp.concatenate([summed, summed_across], axis=1),
    )
    half_beside = swap(half, "tensor", 1)
    whole = jnp.where(
        core_at == 1,
        jnp.concatenate([half_beside, half], axis=1),
        jnp.concatenate([half, half_beside], axis=1),
    )
    return whole[None]


def shards(key_value_rows, queries, w_comp, latent_gain, w_up, w_out, replica_order):
    orders = list(itertools.permutations(range(lax.axis_size("rep"))))
    index = order_index(replica_order, orders)
    query = route(queries[0], index, orders, False)
    rows = key_value_rows[0]
    latent = compress(rows.reshape(rows.shape[0], -1), w_comp, latent_gain)
    latent = lax.all_gather(latent, "tensor", axis=0, tiled=True)
    groups = w_up.shape[0]
    lifted = jnp.einsum("tf,gfy->tgy", latent, w_up, preferred_element_type=F32).astype(BF16)
    head_size = query.shape[-1]
    new_count = query.shape[0]
    keys = lifted[..., :head_size]
    values = lifted[..., head_size:]
    grouped_heads = query.reshape(new_count, groups, -1, head_size)
    scores = jnp.einsum(
        "nghd,tgd->nght", grouped_heads, keys, preferred_element_type=F32
    ) * head_size ** (-0.5)
    top = lax.pmax(jnp.max(scores, axis=-1), "seq")
    expo = jnp.exp(scores - top[..., None])
    total = jnp.sum(expo, axis=-1)
    summed = jnp.einsum("nght,tgd->nghd", expo.astype(BF16), values, preferred_element_type=F32)
    summed, total = lax.psum((summed, total), "seq")
    attended = (summed / total[..., None]).astype(BF16).reshape(new_count, -1)
    attended = route(attended, index, orders, True)
    return lax.psum(dot(attended, w_out), "tensor").astype(BF16)[None]


def solution(mesh):
    placed = (
        P("rep", ("seq", "tensor"), None, None),
        P("rep", None, "tensor", None),
        P(),
        P(),
        P("tensor", None, None),
        P("tensor", "seq"),
        P(),
    )
    square = mesh.shape["seq"] == 2 and mesh.shape["tensor"] == 4
    return jax.shard_map(
        square_shards if square else shards,
        mesh=mesh,
        in_specs=placed,
        out_specs=P("rep", None, "seq"),
        check_vma=False,
    )
```

time: 202 us -> 90.5 us (0.45)
  waiting for transfers between devices: 108 us -> 30.4 us
  blocking collectives: 37 us -> 0 us
  local copies, waits for them, and re-layouts: 4.22 us -> 28.5 us
  matrix products: 22.2 us -> 0 us
  Pallas kernels: 0 us -> 14.8 us
  between operations: 13.2 us -> 0.83 us
  other arithmetic: 12.8 us -> 1.12 us
  starting transfers between devices: 4.46 us -> 14.3 us
    all_gather x3 -> x0, waiting for transfers between devices: 87.3 us -> none  [the longest x1 43.4 us: shards(): piece = lax.all_gather(mixed, 'rep', axis=0, tiled=True)]
    psum x2 -> x0, blocking collectives: 32 us -> none  [the longest x1 26.9 us: shards(): mixed = lax.psum(partial_output, 'tensor').astype(jnp.bfloat16)[None]]
    ppermute x0 -> x14, waiting for transfers between devices: none -> 30.4 us  [the longest x9 13.9 us: swap(): return lax.ppermute(value, axis, pairs)]
    unnamed x9 -> x18, local copies, waits for them, and re-layouts: 1.91 us -> 27.7 us
    dot_general x5 -> x0, matrix products: 22.2 us -> none  [the longest x1 8.78 us: shards(): jnp.dot(attended_values, w_out, preferred_element_type=jnp.float32)]
    psum x1 -> x0, waiting for transfers between devices: 19.2 us -> none  [shards(): summed, total = lax.psum((summed, total), 'seq')]
    pallas_call x0 -> x8, Pallas kernels: none -> 14.8 us  [call(): pl.pallas_call(body, out_shape=outs, in_specs=specs, out_specs=out_specs,...]
    ppermute x0 -> x14, starting transfers between devices: none -> 14.3 us  [the longest x3 6.04 us: cross(): return lax.ppermute(value, ('seq', 'tensor'), pairs)]
  transfers between devices with their start and end apart: 5 -> 14, of which waited for: 4 -> 7; matrix products, arithmetic and copies ran while one was open for 8% -> 0% of each run, Pallas kernels for 0% -> 10%
where the time goes in v2:
time: 90.5 us; the launch traced here: 90 us
  waiting for transfers between devices  30.4 us (34%)
  local copies, waits for them, and re-layouts  28.5 us (31%)
  Pallas kernels  14.8 us (16%)
  starting transfers between devices  14.3 us (16%)
  other arithmetic  1.12 us (1%)
    unnamed x18, local copies, waits for them, and re-layouts  27.7 us
    pallas_call x8, Pallas kernels, call(): pl.pallas_call(body, out_shape=outs, in_specs=specs, out_specs=out_specs,...  14.8 us
    ppermute x9, waiting for transfers between devices, swap(): return lax.ppermute(value, axis, pairs)  13.9 us
    ppermute x3, waiting for transfers between devices, cross(): return lax.ppermute(value, ('seq', 'tensor'), pairs)  7.79 us
    ppermute x3, starting transfers between devices, cross(): return lax.ppermute(value, ('seq', 'tensor'), pairs)  6.04 us
    ppermute x1, waiting for transfers between devices, run(): lax.ppermute(query, 'rep', route_pairs(order, False))  4.44 us
    ppermute x1, waiting for transfers between devices, branch(): return lambda v: lax.ppermute(v, 'rep', route_pairs(order, back))  4.28 us
    ppermute x9, starting transfers between devices, swap(): return lax.ppermute(value, axis, pairs)  4.12 us
  transfers between devices with their start and end apart: 14, of which 7 were waited for; matrix products, arithmetic and copies ran while one was open for 0% of the time, Pallas kernels for 10%

profile of v2, /device:TPU:0, one launch (start us, length us, event | category | flops | bytes accessed | tf_op | source)
XLA Modules:
  0.0 90.0 jit_solution(489876745832194862)
XLA Ops:
  0.0 0.7 broadcast_in_dim.4.gain_ref
  0.7 1.6 %copy-done.5 = bf16[2048,512]{1,0:T(8,128)(2,1)S(1)} copy-done((bf16[2048,512]{1,0:T(8,128)(2,1)S(1)}, bf16[2048,512]{1,0:T(8,128)(2,1)}, u32[]{:S(2)}) %copy-start.5) | copy-done | bytes 2097176
  2.3 1.4 %copy-done.6 = bf16[1,384,8,256]{3,2,1,0:T(8,128)(2,1)S(1)} copy-done((bf16[1,384,8,256]{3,2,1,0:T(8,128)(2,1)S(1)}, bf16[1,384,8,256]{3,2,1,0:T(8,128)(2,1)}, u32[]{:S(2)}) %copy-start.6) | copy-done | bytes 1572888
  3.7 0.9 %copy-done.7 = bf16[1,64,16,128]{3,2,1,0:T(8,128)(2,1)S(1)} copy-done((bf16[1,64,16,128]{3,2,1,0:T(8,128)(2,1)S(1)}, bf16[1,64,16,128]{3,2,1,0:T(8,128)(2,1)}, u32[]{:S(2)}) %copy-start.7) | copy-done | bytes 262168
  4.7 0.7 copy-done.8
  5.3 2.1 %compress.1 = (bf16[384,512]{1,0:T(8,128)(2,1)S(1)}, bf16[512,128]{1,0:T(8,128)(2,1)S(1)}, s32[1]{0:T(128)}) custom-call(s32[4]{0:T(128)S(1)} %copy-done.8, bf16[384,8,256]{2,1,0:T(8,128)(2,1)S(1)} %bitcast.5, bf16[2048,512]{1,0:T(8,128)(2,1)S(1)} %copy-done.5, bf16[1,512]{1,0:T(2,128)(2,1)S(1)} %broadcast_in_dim.4.gain_ref, bf16[64,16,128]{2,1,0:T(8,128)(2,1)S(1)} %bitcast.6), custom_call_target="tpu_custom_call" | custom-call | flops 805306368 | bytes 1572864 | tf_op jit(solution)/shard_map/compress/pallas_call | solution.py:28
  8.2 12.6 %conditional.2 = (bf16[384,512]{1,0:T(8,128)(2,1)}, bf16[384,512]{1,0:T(8,128)(2,1)}, bf16[384,512]{1,0:T(8,128)(2,1)}, bf16[512,128]{1,0:T(8,128)(2,1)}) conditional(s32[]{:T(128)} %bitcast.2, (bf16[384,512]{1,0:T(8,128)(2,1)S(1)}, bf16[512,128]{1,0:T(8,128)(2,1)S(1)}) %tuple.173, (bf16[384,512]{1,0:T(8,128)(2,1)S(1)}, ...), branch_computations={%region_0.1_spmd, %region_1.2_spmd, %region_2.3_spmd, %region_3.4_... | conditional | bytes 5243072 | solution.py:261
  8.2 3.0 %collective-permute-start.28 = (bf16[384,512]{1,0:T(8,128)(2,1)S(1)}, bf16[384,512]{1,0:T(8,128)(2,1)}, u32[]{:S(2)}, u32[]{:S(2)}) collective-permute-start(bf16[384,512]{1,0:T(8,128)(2,1)S(1)} %get-tuple-element.164), channel_id=1, source_target_pairs={{0,16},{1,3},{2,18},{3,1},{16,0},{17,19},{18,2},{19,17},{4,20},{5,... | collective-permute-start | bytes 1179656 | tf_op jit(solution)/shard_map/cond/branch_7_fun/ppermute | solution.py:78
  11.2 1.5 %collective-permute-start.29 = (bf16[384,512]{1,0:T(8,128)(2,1)S(1)}, bf16[384,512]{1,0:T(8,128)(2,1)}, u32[]{:S(2)}, u32[]{:S(2)}) collective-permute-start(bf16[384,512]{1,0:T(8,128)(2,1)S(1)} %get-tuple-element.164), channel_id=1, source_target_pairs={{0,2},{1,17},{2,0},{3,19},{16,18},{17,1},{18,16},{19,3},{4,6},{5,2... | collective-permute-start | bytes 1179656 | tf_op jit(solution)/shard_map/cond/branch_7_fun/ppermute | solution.py:78
  12.7 0.0 collective-permute-start.30
  12.7 1.6 %collective-permute-start.31 = (bf16[512,128]{1,0:T(8,128)(2,1)S(1)}, bf16[512,128]{1,0:T(8,128)(2,1)}, u32[]{:S(2)}, u32[]{:S(2)}) collective-permute-start(bf16[512,128]{1,0:T(8,128)(2,1)S(1)} %get-tuple-element.165), channel_id=1, source_target_pairs={{0,4},{4,0},{8,12},{12,8},{1,5},{5,1},{9,13},{13,9},{2,6},{6,2},{1... | collective-permute-start | bytes 393224 | tf_op jit(solution)/shard_map/cond/branch_7_fun/ppermute | solution.py:256
  14.3 4.4 %collective-permute-done.31 = bf16[512,128]{1,0:T(8,128)(2,1)} collective-permute-done((bf16[512,128]{1,0:T(8,128)(2,1)S(1)}, bf16[512,128]{1,0:T(8,128)(2,1)}, u32[]{:S(2)}, u32[]{:S(2)}) %collective-permute-start.31) | collective-permute-done | bytes 131104 | tf_op jit(solution)/shard_map/cond/branch_7_fun/ppermute | solution.py:256
  18.7 2.0 %collective-permute-done.28 = bf16[384,512]{1,0:T(8,128)(2,1)} collective-permute-done((bf16[384,512]{1,0:T(8,128)(2,1)S(1)}, bf16[384,512]{1,0:T(8,128)(2,1)}, u32[]{:S(2)}, u32[]{:S(2)}) %collective-permute-start.28) | collective-permute-done | bytes 393248 | tf_op jit(solution)/shard_map/cond/branch_7_fun/ppermute | solution.py:78
  20.8 0.0 collective-permute-done.29
  20.8 0.0 collective-permute-done.30
  20.8 1.5 %collective-permute-start.122 = (bf16[384,512]{1,0:T(8,128)(2,1)}, bf16[384,512]{1,0:T(8,128)(2,1)S(1)}, u32[]{:S(2)}, u32[]{:S(2)}) collective-permute-start(bf16[384,512]{1,0:T(8,128)(2,1)} %get-tuple-element.223.refs_0_), channel_id=1, source_target_pairs={{0,2},{1,17},{2,0},{3,19},{16,18},{17,1},{18,16},{19,3},{4,6},{5,2... | collective-permute-start | bytes 1179656 | tf_op jit(solution)/shard_map/ppermute | solution.py:78
  22.3 0.8 collective-permute-start.120
  23.1 5.7 %collective-permute-done.122.refs_0_ = bf16[384,512]{1,0:T(8,128)(2,1)S(1)} collective-permute-done((bf16[384,512]{1,0:T(8,128)(2,1)}, bf16[384,512]{1,0:T(8,128)(2,1)S(1)}, u32[]{:S(2)}, u32[]{:S(2)}) %collective-permute-start.122) | collective-permute-done | bytes 393248 | tf_op jit(solution)/shard_map/ppermute | solution.py:78
  28.8 0.0 collective-permute-start.123
  28.8 5.8 %copy-done.3 = bf16[2048,4096]{1,0:T(8,128)(2,1)S(1)} copy-done((bf16[2048,4096]{1,0:T(8,128)(2,1)S(1)}, bf16[2048,4096]{1,0:T(8,128)(2,1)}, u32[]{:S(2)}) %copy-start.3) | copy-done | bytes 16777240
  34.6 3.0 %score_chip.1 = (f32[768,512]{1,0:T(8,128)S(1)}, bf16[768,128]{1,0:T(8,128)(2,1)S(1)}, f32[8,512]{1,0:T(8,128)S(1)}, bf16[2048,4096]{1,0:T(8,128)(2,1)S(1)}) custom-call(bf16[384,512]{1,0:T(8,128)(2,1)S(1)} %get-tuple-element.216.refs_0_, bf16[384,512]{1,0:T(8,128)(2,1)} %get-tuple-element.218.refs_1_, bf16[2,512,256]{2,1,0:T(8,128)(2,1)S(1)} %copy-done.4, ...), custom_call_target="tpu_custom_call" | custom-call | flops 301989888 | bytes 16777216 | tf_op jit(solution)/shard_map/score_chip/pallas_call | solution.py:28
  37.6 5.8 %copy-done = bf16[2048,4096]{1,0:T(8,128)(2,1)} copy-done((bf16[2048,4096]{1,0:T(8,128)(2,1)}, bf16[2048,4096]{1,0:T(8,128)(2,1)S(1)}, u32[]{:S(2)}) %copy-start) | copy-done | bytes 16777240
  43.5 0.0 collective-permute-done.120.refs_1_
  43.5 2.3 %score_next.1 = (f32[1536,512]{1,0:T(8,128)S(1)}, bf16[1536,128]{1,0:T(8,128)(2,1)S(1)}, f32[8,512]{1,0:T(8,128)S(1)}) custom-call(bf16[384,512]{1,0:T(8,128)(2,1)} %get-tuple-element.223.refs_0_, bf16[384,512]{1,0:T(8,128)(2,1)S(1)} %collective-permute-done.120.refs_1_, bf16[384,512]{1,0:T(8,128)(2,1)} %get-tuple-element.224.refs_2_, ...), custom_call_target="tpu_custom_call" | custom-call | flops 603979776 | bytes 4718592 | tf_op jit(solution)/shard_map/score_next/pallas_call | solution.py:28
  45.8 0.0 collective-permute-done.123.refs_1_
  45.8 1.7 %score_corner.1 = (f32[768,512]{1,0:T(8,128)S(1)}, bf16[768,128]{1,0:T(8,128)(2,1)S(1)}, f32[8,512]{1,0:T(8,128)S(1)}) custom-call(bf16[384,512]{1,0:T(8,128)(2,1)S(1)} %collective-permute-done.122.refs_0_, bf16[384,512]{1,0:T(8,128)(2,1)S(1)} %collective-permute-done.123.refs_1_, bf16[2,512,256]{2,1,0:T(8,128)(2,1)S(1)} %copy-done.4, ...), custom_call_target="tpu_custom_call" | custom-call | flops 301989888 | bytes 2359296 | tf_op jit(solution)/shard_map/score_corner/pallas_call | solution.py:28
  47.5 1.4 %attend.1 = bf16[64,1024]{1,0:T(8,128)(2,1)S(1)} custom-call(f32[768,512]{1,0:T(8,128)S(1)} %get-tuple-element.220.refs_0_, bf16[768,128]{1,0:T(8,128)(2,1)S(1)} %get-tuple-element.221.refs_1_, f32[8,512]{1,0:T(8,128)S(1)} %get-tuple-element.222.refs_2_, f32[1536,512]{1,0:T(8,128)S(1)} %get-tuple-element.225.refs_3_, ...), custom_call_target="tpu_custom_call" | custom-call | flops 402653184 | bytes 6291456 | tf_op jit(solution)/shard_map/attend/pallas_call | solution.py:28
  49.0 6.9 %conditional.3 = (bf16[64,1024]{1,0:T(8,128)(2,1)}) conditional(s32[]{:T(128)} %bitcast.2, bf16[64,1024]{1,0:T(8,128)(2,1)S(1)} %attend.1, bf16[64,1024]{1,0:T(8,128)(2,1)S(1)} %attend.1, bf16[64,1024]{1,0:T(8,128)(2,1)S(1)} %attend.1, bf16[64,1024]{1,0:T(8,128)(2,1)S(1)} %attend.1, ...), branch_computations={%region_24.25_spmd, %region_25.26_spmd, %region_26.27_spmd, %regio... | conditional | bytes 524336 | solution.py:68
  49.0 2.6 %collective-permute-start.103 = (bf16[64,1024]{1,0:T(8,128)(2,1)S(1)}, bf16[64,1024]{1,0:T(8,128)(2,1)}, u32[]{:S(2)}, u32[]{:S(2)}) collective-permute-start(bf16[64,1024]{1,0:T(8,128)(2,1)S(1)} %param.31), channel_id=1, source_target_pairs={{4,0},{0,4},{12,8},{8,12},{5,1},{1,5},{13,9},{9,13},{6,2},{2,6},{1... | collective-permute-start | bytes 393224 | tf_op jit(solution)/shard_map/cond/branch_7_fun/ppermute | solution.py:66
  51.6 4.3 %collective-permute-done.103 = bf16[64,1024]{1,0:T(8,128)(2,1)} collective-permute-done((bf16[64,1024]{1,0:T(8,128)(2,1)S(1)}, bf16[64,1024]{1,0:T(8,128)(2,1)}, u32[]{:S(2)}, u32[]{:S(2)}) %collective-permute-start.103) | collective-permute-done | bytes 131104 | tf_op jit(solution)/shard_map/cond/branch_7_fun/ppermute | solution.py:66
  55.9 1.7 %collective-permute-start.124 = (bf16[64,1024]{1,0:T(8,128)(2,1)}, bf16[64,1024]{1,0:T(8,128)(2,1)S(1)}, u32[]{:S(2)}, u32[]{:S(2)}) collective-permute-start(bf16[64,1024]{1,0:T(8,128)(2,1)} %get-tuple-element.328.refs_0_), channel_id=1, source_target_pairs={{0,16},{16,0},{1,17},{17,1},{2,18},{18,2},{3,19},{19,3},{4,20},{20... | collective-permute-start | bytes 393224 | tf_op jit(solution)/shard_map/ppermute | solution.py:73
  57.5 5.8 %copy-done.1 = bf16[2048,4096]{1,0:T(8,128)(2,1)S(1)} copy-done((bf16[2048,4096]{1,0:T(8,128)(2,1)S(1)}, bf16[2048,4096]{1,0:T(8,128)(2,1)}, u32[]{:S(2)}) %copy-start.1) | copy-done | bytes 16777240
  63.3 2.5 %project.1.refs_2_ = f32[2,64,2048]{2,1,0:T(8,128)S(1)} custom-call(bf16[64,1024]{1,0:T(8,128)(2,1)} %get-tuple-element.328.refs_0_, bf16[2048,4096]{1,0:T(8,128)(2,1)S(1)} %copy-done.1), custom_call_target="tpu_custom_call" | custom-call | flops 536870912 | bytes 8388608 | tf_op jit(solution)/shard_map/project/pallas_call | solution.py:28
  65.8 0.0 collective-permute-done.124.refs_0_
  65.8 0.9 project_sent.1
  66.6 0.1 collective-permute-start.125
  66.7 5.8 %copy-done.2 = bf16[2048,4096]{1,0:T(8,128)(2,1)S(1)} copy-done((bf16[2048,4096]{1,0:T(8,128)(2,1)S(1)}, bf16[2048,4096]{1,0:T(8,128)(2,1)}, u32[]{:S(2)}) %copy-start.2) | copy-done | bytes 16777240
  72.5 0.8 project_own.1
  73.4 0.0 collective-permute-done.125
  73.4 0.1 add.12
  73.5 0.8 collective-permute-start.126
  74.2 8.0 %collective-permute-done.126 = f32[64,1024]{1,0:T(8,128)S(1)} collective-permute-done((f32[64,1024]{1,0:T(8,128)S(1)}, f32[64,1024]{1,0:T(8,128)S(1)}, u32[]{:S(2)}, u32[]{:S(2)}) %collective-permute-start.126) | collective-permute-done | bytes 262176 | tf_op jit(solution)/shard_map/ppermute | solution.py:73
  82.3 0.8 collective-permute-start.127
  83.0 4.4 %collective-permute-done.127 = bf16[64,1024]{1,0:T(8,128)(2,1)S(1)} collective-permute-done((bf16[64,1024]{1,0:T(8,128)(2,1)S(1)}, bf16[64,1024]{1,0:T(8,128)(2,1)S(1)}, u32[]{:S(2)}, u32[]{:S(2)}) %collective-permute-start.127) | collective-permute-done | bytes 131104 | tf_op jit(solution)/shard_map/ppermute | solution.py:73
  87.4 0.1 maximum_select_fusion.1
  87.5 0.1 collective-permute-start.128
  87.6 1.5 %collective-permute-done.128 = bf16[64,2048]{1,0:T(8,128)(2,1)S(1)} collective-permute-done((bf16[64,2048]{1,0:T(8,128)(2,1)S(1)}, bf16[64,2048]{1,0:T(8,128)(2,1)S(1)}, u32[]{:S(2)}, u32[]{:S(2)}) %collective-permute-start.128) | collective-permute-done | bytes 262176 | tf_op jit(solution)/shard_map/ppermute | solution.py:73
  89.1 0.9 %maximum_select_fusion = bf16[1,64,4096]{2,1,0:T(8,128)(2,1)} fusion(bf16[1,64,2048]{2,1,0:T(8,128)(2,1)S(1)} %bitcast.7, bf16[1,64,2048]{2,1,0:T(8,128)(2,1)S(1)} %bitcast.8, pred[]{:T(512)S(6)} %eq.8), kind=kLoop, calls=%fused_computation | loop fusion | flops 2359296 | bytes 1048577 | tf_op jit(solution)/shard_map/jit(_where)/select_n | solution.py:317
  (14 shorter events, 0.1 us)
Async XLA Ops:
  0.0 28.8 %copy-start.4 = (bf16[2,512,256]{2,1,0:T(8,128)(2,1)S(1)}, bf16[2,512,256]{2,1,0:T(8,128)(2,1)}, u32[]{:S(2)}) copy-start(bf16[2,512,256]{2,1,0:T(8,128)(2,1)} %refs_2_.3) | copy-start | bytes 1572868
  0.7 1.6 %copy-start.5 = (bf16[2048,512]{1,0:T(8,128)(2,1)S(1)}, bf16[2048,512]{1,0:T(8,128)(2,1)}, u32[]{:S(2)}) copy-start(bf16[2048,512]{1,0:T(8,128)(2,1)} %weight_ref.1) | copy-start | bytes 6291460
  2.3 1.4 %copy-start.6 = (bf16[1,384,8,256]{3,2,1,0:T(8,128)(2,1)S(1)}, bf16[1,384,8,256]{3,2,1,0:T(8,128)(2,1)}, u32[]{:S(2)}) copy-start(bf16[1,384,8,256]{3,2,1,0:T(8,128)(2,1)} %param.55) | copy-start | bytes 4718596
  3.7 0.9 %copy-start.7 = (bf16[1,64,16,128]{3,2,1,0:T(8,128)(2,1)S(1)}, bf16[1,64,16,128]{3,2,1,0:T(8,128)(2,1)}, u32[]{:S(2)}) copy-start(bf16[1,64,16,128]{3,2,1,0:T(8,128)(2,1)} %param.56) | copy-start | bytes 786436
  4.7 0.7 copy-start.8
  8.2 12.6 %collective-permute-start.28 = (bf16[384,512]{1,0:T(8,128)(2,1)S(1)}, bf16[384,512]{1,0:T(8,128)(2,1)}, u32[]{:S(2)}, u32[]{:S(2)}) collective-permute-start(bf16[384,512]{1,0:T(8,128)(2,1)S(1)} %get-tuple-element.164), channel_id=1, source_target_pairs={{0,16},{1,3},{2,18},{3,1},{16,0},{17,19},{18,2},{19,17},{4,20},{5,... | collective-permute-start | bytes 1179656 | tf_op jit(solution)/shard_map/cond/branch_7_fun/ppermute | solution.py:78
  11.2 9.6 %collective-permute-start.29 = (bf16[384,512]{1,0:T(8,128)(2,1)S(1)}, bf16[384,512]{1,0:T(8,128)(2,1)}, u32[]{:S(2)}, u32[]{:S(2)}) collective-permute-start(bf16[384,512]{1,0:T(8,128)(2,1)S(1)} %get-tuple-element.164), channel_id=1, source_target_pairs={{0,2},{1,17},{2,0},{3,19},{16,18},{17,1},{18,16},{19,3},{4,6},{5,2... | collective-permute-start | bytes 1179656 | tf_op jit(solution)/shard_map/cond/branch_7_fun/ppermute | solution.py:78
  12.7 8.1 %collective-permute-start.30 = (bf16[384,512]{1,0:T(8,128)(2,1)S(1)}, bf16[384,512]{1,0:T(8,128)(2,1)}, u32[]{:S(2)}, u32[]{:S(2)}) collective-permute-start(bf16[384,512]{1,0:T(8,128)(2,1)S(1)} %get-tuple-element.164), channel_id=1, source_target_pairs={{0,1},{1,0},{2,3},{3,2},{4,5},{5,4},{6,7},{7,6},{8,9},{9,8},{10,11... | collective-permute-start | bytes 1179656 | tf_op jit(solution)/shard_map/cond/branch_7_fun/ppermute | solution.py:73
  12.7 6.0 %collective-permute-start.31 = (bf16[512,128]{1,0:T(8,128)(2,1)S(1)}, bf16[512,128]{1,0:T(8,128)(2,1)}, u32[]{:S(2)}, u32[]{:S(2)}) collective-permute-start(bf16[512,128]{1,0:T(8,128)(2,1)S(1)} %get-tuple-element.165), channel_id=1, source_target_pairs={{0,4},{4,0},{8,12},{12,8},{1,5},{5,1},{9,13},{13,9},{2,6},{6,2},{1... | collective-permute-start | bytes 393224 | tf_op jit(solution)/shard_map/cond/branch_7_fun/ppermute | solution.py:256
  20.8 8.0 %collective-permute-start.122 = (bf16[384,512]{1,0:T(8,128)(2,1)}, bf16[384,512]{1,0:T(8,128)(2,1)S(1)}, u32[]{:S(2)}, u32[]{:S(2)}) collective-permute-start(bf16[384,512]{1,0:T(8,128)(2,1)} %get-tuple-element.223.refs_0_), channel_id=1, source_target_pairs={{0,2},{1,17},{2,0},{3,19},{16,18},{17,1},{18,16},{19,3},{4,6},{5,2... | collective-permute-start | bytes 1179656 | tf_op jit(solution)/shard_map/ppermute | solution.py:78
  22.3 21.2 %collective-permute-start.120 = (bf16[384,512]{1,0:T(8,128)(2,1)}, bf16[384,512]{1,0:T(8,128)(2,1)S(1)}, u32[]{:S(2)}, u32[]{:S(2)}) collective-permute-start(bf16[384,512]{1,0:T(8,128)(2,1)} %get-tuple-element.223.refs_0_), channel_id=1, source_target_pairs={{0,1},{1,0},{2,3},{3,2},{4,5},{5,4},{6,7},{7,6},{8,9},{9,8},{10,11... | collective-permute-start | bytes 1179656 | tf_op jit(solution)/shard_map/ppermute | solution.py:73
  23.1 20.4 %collective-permute-start.121 = (bf16[384,512]{1,0:T(8,128)(2,1)}, bf16[384,512]{1,0:T(8,128)(2,1)S(1)}, u32[]{:S(2)}, u32[]{:S(2)}) collective-permute-start(bf16[384,512]{1,0:T(8,128)(2,1)} %get-tuple-element.224.refs_2_), channel_id=1, source_target_pairs={{0,1},{1,0},{2,3},{3,2},{4,5},{5,4},{6,7},{7,6},{8,9},{9,8},{10,11... | collective-permute-start | bytes 1179656 | tf_op jit(solution)/shard_map/ppermute | solution.py:73
  28.8 17.0 %collective-permute-start.123 = (bf16[384,512]{1,0:T(8,128)(2,1)S(1)}, bf16[384,512]{1,0:T(8,128)(2,1)S(1)}, u32[]{:S(2)}, u32[]{:S(2)}) collective-permute-start(bf16[384,512]{1,0:T(8,128)(2,1)S(1)} %collective-permute-done.122.refs_0_), channel_id=1, source_target_pairs={{0,1},{1,0},{2,3},{3,2},{4,5},{5,4},{6,7},{7,6},{8,9},{9,8},{10,11... | collective-permute-start | bytes 1179656 | tf_op jit(solution)/shard_map/ppermute | solution.py:73
  28.8 5.8 %copy-start.3 = (bf16[2048,4096]{1,0:T(8,128)(2,1)S(1)}, bf16[2048,4096]{1,0:T(8,128)(2,1)}, u32[]{:S(2)}) copy-start(bf16[2048,4096]{1,0:T(8,128)(2,1)} %refs_4_.2) | copy-start | bytes 50331652
  37.6 5.8 %copy-start = (bf16[2048,4096]{1,0:T(8,128)(2,1)}, bf16[2048,4096]{1,0:T(8,128)(2,1)S(1)}, u32[]{:S(2)}) copy-start(bf16[2048,4096]{1,0:T(8,128)(2,1)S(1)} %get-tuple-element.231.refs_1_) | copy-start | bytes 50331652
  49.0 6.9 %collective-permute-start.103 = (bf16[64,1024]{1,0:T(8,128)(2,1)S(1)}, bf16[64,1024]{1,0:T(8,128)(2,1)}, u32[]{:S(2)}, u32[]{:S(2)}) collective-permute-start(bf16[64,1024]{1,0:T(8,128)(2,1)S(1)} %param.31), channel_id=1, source_target_pairs={{4,0},{0,4},{12,8},{8,12},{5,1},{1,5},{13,9},{9,13},{6,2},{2,6},{1... | collective-permute-start | bytes 393224 | tf_op jit(solution)/shard_map/cond/branch_7_fun/ppermute | solution.py:66
  55.9 9.9 %collective-permute-start.124 = (bf16[64,1024]{1,0:T(8,128)(2,1)}, bf16[64,1024]{1,0:T(8,128)(2,1)S(1)}, u32[]{:S(2)}, u32[]{:S(2)}) collective-permute-start(bf16[64,1024]{1,0:T(8,128)(2,1)} %get-tuple-element.328.refs_0_), channel_id=1, source_target_pairs={{0,16},{16,0},{1,17},{17,1},{2,18},{18,2},{3,19},{19,3},{4,20},{20... | collective-permute-start | bytes 393224 | tf_op jit(solution)/shard_map/ppermute | solution.py:73
  57.5 5.8 %copy-start.1 = (bf16[2048,4096]{1,0:T(8,128)(2,1)S(1)}, bf16[2048,4096]{1,0:T(8,128)(2,1)}, u32[]{:S(2)}) copy-start(bf16[2048,4096]{1,0:T(8,128)(2,1)} %copy-done) | copy-start | bytes 50331652
  66.6 6.7 %collective-permute-start.125 = (f32[64,2048]{1,0:T(8,128)S(1)}, f32[64,2048]{1,0:T(8,128)S(1)}, u32[]{:S(2)}, u32[]{:S(2)}) collective-permute-start(f32[64,2048]{1,0:T(8,128)S(1)} %project_sent.1), channel_id=1, source_target_pairs={{0,1},{1,0},{2,3},{3,2},{4,5},{5,4},{6,7},{7,6},{8,9},{9,8},{10,11... | collective-permute-start | bytes 1572872 | tf_op jit(solution)/shard_map/ppermute | solution.py:73
  66.7 5.8 %copy-start.2 = (bf16[2048,4096]{1,0:T(8,128)(2,1)S(1)}, bf16[2048,4096]{1,0:T(8,128)(2,1)}, u32[]{:S(2)}) copy-start(bf16[2048,4096]{1,0:T(8,128)(2,1)} %copy-done) | copy-start | bytes 50331652
  73.5 8.8 %collective-permute-start.126 = (f32[64,1024]{1,0:T(8,128)S(1)}, f32[64,1024]{1,0:T(8,128)S(1)}, u32[]{:S(2)}, u32[]{:S(2)}) collective-permute-start(f32[64,1024]{1,0:T(8,128)S(1)} %slice_select_fusion), channel_id=1, source_target_pairs={{0,2},{1,3},{2,0},{3,1},{4,6},{5,7},{6,4},{7,5},{8,10},{9,11},{10,... | collective-permute-start | bytes 786440 | tf_op jit(solution)/shard_map/ppermute | solution.py:73
  82.3 5.2 %collective-permute-start.127 = (bf16[64,1024]{1,0:T(8,128)(2,1)S(1)}, bf16[64,1024]{1,0:T(8,128)(2,1)S(1)}, u32[]{:S(2)}, u32[]{:S(2)}) collective-permute-start(bf16[64,1024]{1,0:T(8,128)(2,1)S(1)} %add_convert_fusion), channel_id=1, source_target_pairs={{0,2},{1,3},{2,0},{3,1},{4,6},{5,7},{6,4},{7,5},{8,10},{9,11},{10,... | collective-permute-start | bytes 393224 | tf_op jit(solution)/shard_map/ppermute | solution.py:73
  87.5 1.6 %collective-permute-start.128 = (bf16[64,2048]{1,0:T(8,128)(2,1)S(1)}, bf16[64,2048]{1,0:T(8,128)(2,1)S(1)}, u32[]{:S(2)}, u32[]{:S(2)}) collective-permute-start(bf16[64,2048]{1,0:T(8,128)(2,1)S(1)} %maximum_select_fusion.1), channel_id=1, source_target_pairs={{0,1},{1,0},{2,3},{3,2},{4,5},{5,4},{6,7},{7,6},{8,9},{9,8},{10,11... | collective-permute-start | bytes 786440 | tf_op jit(solution)/shard_map/ppermute | solution.py:73

commit v3 on v2

--- a/solution.py
+++ b/solution.py
@@ -12,7 +12,7 @@
 MIB = 1024 * 1024
 IN_VMEM = pl.BlockSpec(memory_space=pltpu.VMEM)
 IN_SMEM = pl.BlockSpec(memory_space=pltpu.SMEM)
-ANYWHERE = pl.BlockSpec(memory_space=pl.ANY)
+IN_HBM = pl.BlockSpec(memory_space=pltpu.HBM)
 COPIES = 8
 
 
@@ -20,8 +20,13 @@
     return jax.ShapeDtypeStruct(dims, dtype)
 
 
-def call(body, name, outs, operands, vmem, scratch=(), smem_in=0, smem_out=False, any_in=0, cost=None):
-    specs = [IN_SMEM] * smem_in + [IN_VMEM] * (len(operands) - smem_in - any_in) + [ANYWHERE] * any_in
+def call(body, name, outs, operands, vmem, scratch=(), smem_out=False, hbm_in=0, cost=None):
+    kept = len(operands) - hbm_in
+    specs = [IN_VMEM] * kept + [IN_HBM] * hbm_in
+    operands = [
+        *operands[:kept],
+        *(pltpu.with_memory_space_constraint(operand, pltpu.HBM) for operand in operands[kept:]),
+    ]
     out_specs = [IN_VMEM] * len(outs)
     if smem_out:
         out_specs[-1] = IN_SMEM
@@ -78,28 +83,26 @@
     return lax.ppermute(value, ("seq", "tensor"), pairs)
 
 
-def compress_kernel(order_ref, rows_ref, weight_ref, gain_ref, query_ref, latent_ref, half_ref, index_ref, wide):
+def compress_kernel(chunks, *refs):
+    (order_hbm, rows_hbm, weight_hbm, gain_hbm, query_hbm, latent_ref, half_ref, index_ref) = refs[:8]
+    (order_ref, rows_ref, weight_ref, gain_ref, query_ref, wide, sems) = refs[8:]
     tokens, groups, width = rows_ref.shape
-    lanes = wide.shape[2]
-    for part in range(wide.shape[0]):
-        values = rows_ref[:, :, part * lanes : (part + 1) * lanes].astype(F32)
-        wide[part] = values.reshape(tokens * groups, lanes)
-    projected = jnp.zeros((tokens, weight_ref.shape[1]), F32)
+    chunk = tokens // chunks
+    copies = [pltpu.make_async_copy(order_hbm, order_ref, sems.at[0])]
+    for i in range(chunks):
+        at = pl.ds(i * chunk, chunk)
+        copies.append(pltpu.make_async_copy(rows_hbm.at[0, at], rows_ref.at[at], sems.at[1 + i]))
     for group in range(groups):
-        picked = [
-            wide[part, pl.ds(group, tokens, stride=groups), :] for part in range(wide.shape[0])
-        ]
-        picked = jnp.concatenate(picked, axis=1).astype(BF16)
-        projected += dot(picked, weight_ref[group * width : (group + 1) * width, :])
-    scale = lax.rsqrt(jnp.mean(projected * projected, axis=-1, keepdims=True) + 1e-06)
-    latent_ref[...] = (projected * scale * gain_ref[...].astype(F32)).astype(BF16)
-
-    new_count, heads, head_size = query_ref.shape
-    query = query_ref[...].astype(F32)
-    upper = lax.axis_index("seq") == 1
-    query = jnp.where(upper, query[:, heads // 2 :], query[:, : heads // 2])
-    half_ref[...] = query.reshape(half_ref.shape).astype(BF16)
-
+        at = pl.ds(group * width, width)
+        copies.append(
+            pltpu.make_async_copy(weight_hbm.at[at], weight_ref.at[at], sems.at[1 + chunks + group])
+        )
+    copies.append(pltpu.make_async_copy(gain_hbm, gain_ref, sems.at[1 + chunks + groups]))
+    copies.append(pltpu.make_async_copy(query_hbm.at[0], query_ref, sems.at[2 + chunks + groups]))
+    for copy in copies:
+        copy.start()
+
+    copies[0].wait()
     count = order_ref.shape[0]
     index = 0
     for i in range(count):
@@ -108,6 +111,33 @@
             smaller = smaller + (order_ref[j] < order_ref[i]).astype(jnp.int32)
         index = index + smaller * math.factorial(count - 1 - i)
     index_ref[0] = index
+
+    lanes = wide.shape[2]
+    for i in range(chunks):
+        copies[1 + i].wait()
+        for part in range(wide.shape[0]):
+            values = rows_ref[i * chunk : (i + 1) * chunk, :, part * lanes : (part + 1) * lanes]
+            wide[part, i * chunk * groups : (i + 1) * chunk * groups] = values.astype(F32).reshape(
+                chunk * groups, lanes
+            )
+    projected = jnp.zeros((tokens, weight_ref.shape[1]), F32)
+    for group in range(groups):
+        picked = [
+            wide[part, pl.ds(group, tokens, stride=groups), :] for part in range(wide.shape[0])
+        ]
+        picked = jnp.concatenate(picked, axis=1).astype(BF16)
+        copies[1 + chunks + group].wait()
+        projected += dot(picked, weight_ref[group * width : (group + 1) * width, :])
+    copies[1 + chunks + groups].wait()
+    scale = lax.rsqrt(jnp.mean(projected * projected, axis=-1, keepdims=True) + 1e-06)
+    latent_ref[...] = (projected * scale * gain_ref[...].astype(F32)[None]).astype(BF16)
+
+    copies[2 + chunks + groups].wait()
+    new_count, heads, head_size = query_ref.shape
+    query = query_ref[...].astype(F32)
+    upper = lax.axis_index("seq") == 1
+    query = jnp.where(upper, query[:, heads // 2 :], query[:, : heads // 2])
+    half_ref[...] = query.reshape(half_ref.shape).astype(BF16)
 
 
 def score_kernel(parts, *refs):
@@ -166,7 +196,7 @@
         [*operands, weight],
         12,
         scratch=[pltpu.SemaphoreType.DMA((COPIES,))],
-        any_in=1,
+        hbm_in=1,
         cost=cost(flops, 2 * weight.shape[0] * weight.shape[1]),
     )
 
@@ -235,14 +265,23 @@
     latent_width = w_comp.shape[1]
     rows = heads // 2 * new_count
 
+    chunks = 3 if tokens % 48 == 0 else 1
     latent, query, index = call(
-        compress_kernel,
+        lambda *refs: compress_kernel(chunks, *refs),
         "compress",
         [shape((tokens, latent_width), BF16), shape((rows, head_size), BF16), shape((1,), jnp.int32)],
-        [replica_order, key_value_rows[0], w_comp, latent_gain[None], queries[0]],
+        [replica_order, key_value_rows, w_comp, latent_gain, queries],
         16,
-        scratch=[pltpu.VMEM((width // 128, tokens * all_groups, 128), F32)],
-        smem_in=1,
+        scratch=[
+            pltpu.SMEM(replica_order.shape, jnp.int32),
+            pltpu.VMEM(key_value_rows.shape[1:], BF16),
+            pltpu.VMEM(w_comp.shape, BF16),
+            pltpu.VMEM(latent_gain.shape, BF16),
+            pltpu.VMEM(queries.shape[1:], BF16),
+            pltpu.VMEM((width // 128, tokens * all_groups, 128), F32),
+            pltpu.SemaphoreType.DMA((3 + chunks + all_groups,)),
+        ],
+        hbm_in=5,
         smem_out=True,
         cost=cost(2 * tokens * all_groups * width * latent_width, 2 * tokens * all_groups * width),
     )
@@ -264,6 +303,7 @@
     far_beside = swap(far, "tensor", 1)
     corner_beside = swap(corner, "tensor", 1)
     *first, held = score_call("score_chip", [latent, beside], w_up, query, w_out)
+    held = pltpu.with_memory_space_constraint(held, pltpu.VMEM)
     second = score_call("score_next", [near, near_beside, far, far_beside], w_up, query)
     third = score_call("score_corner", [corner, corner_beside], w_up, query)
     depth = rows // new_count * head_size

time: 90.5 us -> 87.8 us (0.970)
  local copies, waits for them, and re-layouts: 28.5 us -> 17.4 us
  Pallas kernels: 14.8 us -> 20.9 us
  starting transfers between devices: 14.3 us -> 17 us
  waiting for transfers between devices: 30.4 us -> 29.4 us
    unnamed x18 -> x8, local copies, waits for them, and re-layouts: 27.7 us -> 17.4 us
    pallas_call x8, Pallas kernels: 14.8 us -> 20.9 us  [call(): pl.pallas_call(body, out_shape=outs, in_specs=specs, out_specs=out_specs,...]
    ppermute x1, starting transfers between devices: 2.59 us -> 4.51 us  [branch(): return lambda v: lax.ppermute(v, 'rep', route_pairs(order, back))]
    ppermute x1, starting transfers between devices: 1.58 us -> 3.47 us  [run(): lax.ppermute(query, 'rep', route_pairs(order, False))]
    ppermute x3, waiting for transfers between devices: 7.79 us -> 6.76 us  [cross(): return lax.ppermute(value, ('seq', 'tensor'), pairs)]
  transfers between devices with their start and end apart: 14 -> 14, of which waited for: 7 -> 6; matrix products, arithmetic and copies ran while one was open for 0% -> 0% of each run, Pallas kernels for 10% -> 15%
where the time goes in v3:
time: 87.8 us; the launch traced here: 87 us
  waiting for transfers between devices  29.4 us (33%)
  Pallas kernels  20.9 us (24%)
  local copies, waits for them, and re-layouts  17.4 us (20%)
  starting transfers between devices  17 us (19%)
  other arithmetic  1.12 us (1%)
    pallas_call x8, Pallas kernels, call(): pl.pallas_call(body, out_shape=outs, in_specs=specs, out_specs=out_specs,...  20.9 us
    unnamed x8, local copies, waits for them, and re-layouts  17.4 us
    ppermute x9, waiting for transfers between devices, swap(): return lax.ppermute(value, axis, pairs)  14 us
    ppermute x3, waiting for transfers between devices, cross(): return lax.ppermute(value, ('seq', 'tensor'), pairs)  6.76 us
    ppermute x1, waiting for transfers between devices, run(): lax.ppermute(query, 'rep', route_pairs(order, False))  5.32 us
    ppermute x3, starting transfers between devices, cross(): return lax.ppermute(value, ('seq', 'tensor'), pairs)  5.16 us
    ppermute x1, starting transfers between devices, branch(): return lambda v: lax.ppermute(v, 'rep', route_pairs(order, back))  4.51 us
    ppermute x9, starting transfers between devices, swap(): return lax.ppermute(value, axis, pairs)  3.86 us
  transfers between devices with their start and end apart: 14, of which 6 were waited for; matrix products, arithmetic and copies ran while one was open for 0% of the time, Pallas kernels for 15%

profile of v3, /device:TPU:0, one launch (start us, length us, event | category | flops | bytes accessed | tf_op | source)
XLA Modules:
  0.0 87.0 jit_solution(8347953744411402145)
XLA Ops:
  0.0 0.0 copy-start.3
  0.0 4.3 %compress.1 = (bf16[384,512]{1,0:T(8,128)(2,1)S(1)}, bf16[512,128]{1,0:T(8,128)(2,1)S(1)}, s32[1]{0:T(128)}) custom-call(s32[4]{0:T(128)} %refs_0_.1, bf16[1,384,8,256]{3,2,1,0:T(8,128)(2,1)} %refs_1_.1, bf16[2048,512]{1,0:T(8,128)(2,1)} %refs_2_.3, bf16[512]{0:T(512)(128)(2,1)} %refs_3_.1, bf16[1,64,16,128]{3,2,1,0:T(8,128)(2,1)} %refs_4_.3), custom_call_target="tpu_custom_call" | custom-call | flops 805306368 | bytes 1572864 | tf_op jit(solution)/shard_map/compress/pallas_call | solution.py:33
  5.0 13.6 %conditional.2 = (bf16[384,512]{1,0:T(8,128)(2,1)}, bf16[384,512]{1,0:T(8,128)(2,1)}, bf16[384,512]{1,0:T(8,128)(2,1)}, bf16[512,128]{1,0:T(8,128)(2,1)}) conditional(s32[]{:T(128)} %bitcast, (bf16[384,512]{1,0:T(8,128)(2,1)S(1)}, bf16[512,128]{1,0:T(8,128)(2,1)S(1)}) %tuple.173, (bf16[384,512]{1,0:T(8,128)(2,1)S(1)}, ...), branch_computations={%region_0.1_spmd, %region_1.2_spmd, %region_2.3_spmd, %region_3.4_... | conditional | bytes 5243072 | solution.py:300
  5.0 3.0 %collective-permute-start.32 = (bf16[384,512]{1,0:T(8,128)(2,1)S(1)}, bf16[384,512]{1,0:T(8,128)(2,1)}, u32[]{:S(2)}, u32[]{:S(2)}) collective-permute-start(bf16[384,512]{1,0:T(8,128)(2,1)S(1)} %get-tuple-element.166), channel_id=1, source_target_pairs={{0,16},{1,3},{2,18},{3,1},{16,0},{17,19},{18,2},{19,17},{4,20},{5,... | collective-permute-start | bytes 1179656 | tf_op jit(solution)/shard_map/cond/branch_8_fun/ppermute | solution.py:83
  8.1 1.5 %collective-permute-start.33 = (bf16[384,512]{1,0:T(8,128)(2,1)S(1)}, bf16[384,512]{1,0:T(8,128)(2,1)}, u32[]{:S(2)}, u32[]{:S(2)}) collective-permute-start(bf16[384,512]{1,0:T(8,128)(2,1)S(1)} %get-tuple-element.166), channel_id=1, source_target_pairs={{0,2},{1,17},{2,0},{3,19},{16,18},{17,1},{18,16},{19,3},{4,6},{5,2... | collective-permute-start | bytes 1179656 | tf_op jit(solution)/shard_map/cond/branch_8_fun/ppermute | solution.py:83
  9.6 0.0 collective-permute-start.34
  9.6 3.5 %collective-permute-start.35 = (bf16[512,128]{1,0:T(8,128)(2,1)S(1)}, bf16[512,128]{1,0:T(8,128)(2,1)}, u32[]{:S(2)}, u32[]{:S(2)}) collective-permute-start(bf16[512,128]{1,0:T(8,128)(2,1)S(1)} %get-tuple-element.167), channel_id=1, source_target_pairs={{0,4},{4,8},{8,0},{12,12},{1,5},{5,9},{9,1},{13,13},{2,6},{6,10},{... | collective-permute-start | bytes 393224 | tf_op jit(solution)/shard_map/cond/branch_8_fun/ppermute | solution.py:295
  13.1 5.3 %collective-permute-done.35 = bf16[512,128]{1,0:T(8,128)(2,1)} collective-permute-done((bf16[512,128]{1,0:T(8,128)(2,1)S(1)}, bf16[512,128]{1,0:T(8,128)(2,1)}, u32[]{:S(2)}, u32[]{:S(2)}) %collective-permute-start.35) | collective-permute-done | bytes 131104 | tf_op jit(solution)/shard_map/cond/branch_8_fun/ppermute | solution.py:295
  18.4 0.0 collective-permute-done.32
  18.4 0.0 collective-permute-done.33
  18.4 0.0 collective-permute-done.34
  18.6 0.6 collective-permute-start.122
  19.2 0.7 collective-permute-start.120
  19.9 0.0 collective-permute-start.121
  19.9 6.8 %collective-permute-done.122.refs_0_ = bf16[384,512]{1,0:T(8,128)(2,1)S(1)} collective-permute-done((bf16[384,512]{1,0:T(8,128)(2,1)}, bf16[384,512]{1,0:T(8,128)(2,1)S(1)}, u32[]{:S(2)}, u32[]{:S(2)}) %collective-permute-start.122) | collective-permute-done | bytes 393248 | tf_op jit(solution)/shard_map/ppermute | solution.py:83
  26.7 0.0 collective-permute-start.123
  26.7 0.0 copy-done.3
  26.7 7.0 %score_chip.1 = (f32[768,512]{1,0:T(8,128)S(1)}, bf16[768,128]{1,0:T(8,128)(2,1)S(1)}, f32[8,512]{1,0:T(8,128)S(1)}, bf16[2048,4096]{1,0:T(8,128)(2,1)S(1)}) custom-call(bf16[384,512]{1,0:T(8,128)(2,1)S(1)} %get-tuple-element.216.refs_0_, bf16[384,512]{1,0:T(8,128)(2,1)} %get-tuple-element.218.refs_1_, bf16[2,512,256]{2,1,0:T(8,128)(2,1)S(1)} %copy-done.3, ...), custom_call_target="tpu_custom_call" | custom-call | flops 301989888 | bytes 16777216 | tf_op jit(solution)/shard_map/score_chip/pallas_call | solution.py:33
  33.7 0.0 copy-start
  33.7 5.8 %copy-done = bf16[2048,4096]{1,0:T(8,128)(2,1)} copy-done((bf16[2048,4096]{1,0:T(8,128)(2,1)}, bf16[2048,4096]{1,0:T(8,128)(2,1)S(1)}, u32[]{:S(2)}) %copy-start) | copy-done | bytes 16777240
  39.5 0.0 collective-permute-done.120.refs_1_
  39.5 0.0 collective-permute-done.121.refs_3_
  39.5 2.3 %score_next.1 = (f32[1536,512]{1,0:T(8,128)S(1)}, bf16[1536,128]{1,0:T(8,128)(2,1)S(1)}, f32[8,512]{1,0:T(8,128)S(1)}) custom-call(bf16[384,512]{1,0:T(8,128)(2,1)} %get-tuple-element.223.refs_0_, bf16[384,512]{1,0:T(8,128)(2,1)S(1)} %collective-permute-done.120.refs_1_, bf16[384,512]{1,0:T(8,128)(2,1)} %get-tuple-element.224.refs_2_, ...), custom_call_target="tpu_custom_call" | custom-call | flops 603979776 | bytes 4718592 | tf_op jit(solution)/shard_map/score_next/pallas_call | solution.py:33
  41.9 0.0 collective-permute-done.123.refs_1_
  41.9 1.7 %score_corner.1 = (f32[768,512]{1,0:T(8,128)S(1)}, bf16[768,128]{1,0:T(8,128)(2,1)S(1)}, f32[8,512]{1,0:T(8,128)S(1)}) custom-call(bf16[384,512]{1,0:T(8,128)(2,1)S(1)} %collective-permute-done.122.refs_0_, bf16[384,512]{1,0:T(8,128)(2,1)S(1)} %collective-permute-done.123.refs_1_, bf16[2,512,256]{2,1,0:T(8,128)(2,1)S(1)} %copy-done.3, ...), custom_call_target="tpu_custom_call" | custom-call | flops 301989888 | bytes 2359296 | tf_op jit(solution)/shard_map/score_corner/pallas_call | solution.py:33
  43.6 1.4 %attend.1 = bf16[64,1024]{1,0:T(8,128)(2,1)S(1)} custom-call(f32[768,512]{1,0:T(8,128)S(1)} %get-tuple-element.220.refs_0_, bf16[768,128]{1,0:T(8,128)(2,1)S(1)} %get-tuple-element.221.refs_1_, f32[8,512]{1,0:T(8,128)S(1)} %get-tuple-element.222.refs_2_, f32[1536,512]{1,0:T(8,128)S(1)} %get-tuple-element.225.refs_3_, ...), custom_call_target="tpu_custom_call" | custom-call | flops 402653184 | bytes 6291456 | tf_op jit(solution)/shard_map/attend/pallas_call | solution.py:33
  45.0 8.0 %conditional.3 = (bf16[64,1024]{1,0:T(8,128)(2,1)}) conditional(s32[]{:T(128)} %bitcast, bf16[64,1024]{1,0:T(8,128)(2,1)S(1)} %attend.1, bf16[64,1024]{1,0:T(8,128)(2,1)S(1)} %attend.1, bf16[64,1024]{1,0:T(8,128)(2,1)S(1)} %attend.1, bf16[64,1024]{1,0:T(8,128)(2,1)S(1)} %attend.1, ...), branch_computations={%region_24.25_spmd, %region_25.26_spmd, %region_26.27_spmd, %regio... | conditional | bytes 524336 | solution.py:73
  45.0 4.5 %collective-permute-start.104 = (bf16[64,1024]{1,0:T(8,128)(2,1)S(1)}, bf16[64,1024]{1,0:T(8,128)(2,1)}, u32[]{:S(2)}, u32[]{:S(2)}) collective-permute-start(bf16[64,1024]{1,0:T(8,128)(2,1)S(1)} %param.32), channel_id=1, source_target_pairs={{4,0},{8,4},{0,8},{12,12},{5,1},{9,5},{1,9},{13,13},{6,2},{10,6},{... | collective-permute-start | bytes 393224 | tf_op jit(solution)/shard_map/cond/branch_8_fun/ppermute | solution.py:71
  49.5 3.4 %collective-permute-done.104 = bf16[64,1024]{1,0:T(8,128)(2,1)} collective-permute-done((bf16[64,1024]{1,0:T(8,128)(2,1)S(1)}, bf16[64,1024]{1,0:T(8,128)(2,1)}, u32[]{:S(2)}, u32[]{:S(2)}) %collective-permute-start.104) | collective-permute-done | bytes 131104 | tf_op jit(solution)/shard_map/cond/branch_8_fun/ppermute | solution.py:71
  52.9 1.5 %collective-permute-start.124 = (bf16[64,1024]{1,0:T(8,128)(2,1)}, bf16[64,1024]{1,0:T(8,128)(2,1)S(1)}, u32[]{:S(2)}, u32[]{:S(2)}) collective-permute-start(bf16[64,1024]{1,0:T(8,128)(2,1)} %get-tuple-element.328.refs_0_), channel_id=1, source_target_pairs={{0,16},{16,0},{1,17},{17,1},{2,18},{18,2},{3,19},{19,3},{4,20},{20... | collective-permute-start | bytes 393224 | tf_op jit(solution)/shard_map/ppermute | solution.py:78
  54.5 5.8 %copy-done.1 = bf16[2048,4096]{1,0:T(8,128)(2,1)S(1)} copy-done((bf16[2048,4096]{1,0:T(8,128)(2,1)S(1)}, bf16[2048,4096]{1,0:T(8,128)(2,1)}, u32[]{:S(2)}) %copy-start.1) | copy-done | bytes 16777240
  60.2 2.5 %project.1.refs_2_ = f32[2,64,2048]{2,1,0:T(8,128)S(1)} custom-call(bf16[64,1024]{1,0:T(8,128)(2,1)} %get-tuple-element.328.refs_0_, bf16[2048,4096]{1,0:T(8,128)(2,1)S(1)} %copy-done.1), custom_call_target="tpu_custom_call" | custom-call | flops 536870912 | bytes 8388608 | tf_op jit(solution)/shard_map/project/pallas_call | solution.py:33
  62.7 0.0 collective-permute-done.124.refs_0_
  62.7 0.9 project_sent.1
  63.6 0.1 collective-permute-start.125
  63.7 0.0 copy-start.2
  63.7 5.8 %copy-done.2 = bf16[2048,4096]{1,0:T(8,128)(2,1)S(1)} copy-done((bf16[2048,4096]{1,0:T(8,128)(2,1)S(1)}, bf16[2048,4096]{1,0:T(8,128)(2,1)}, u32[]{:S(2)}) %copy-start.2) | copy-done | bytes 16777240
  69.5 0.8 project_own.1
  70.3 0.0 collective-permute-done.125
  70.3 0.1 add.12
  70.4 0.7 collective-permute-start.126
  71.2 8.0 %collective-permute-done.126 = f32[64,1024]{1,0:T(8,128)S(1)} collective-permute-done((f32[64,1024]{1,0:T(8,128)S(1)}, f32[64,1024]{1,0:T(8,128)S(1)}, u32[]{:S(2)}, u32[]{:S(2)}) %collective-permute-start.126) | collective-permute-done | bytes 262176 | tf_op jit(solution)/shard_map/ppermute | solution.py:78
  79.2 0.7 collective-permute-start.127
  80.0 4.4 %collective-permute-done.127 = bf16[64,1024]{1,0:T(8,128)(2,1)S(1)} collective-permute-done((bf16[64,1024]{1,0:T(8,128)(2,1)S(1)}, bf16[64,1024]{1,0:T(8,128)(2,1)S(1)}, u32[]{:S(2)}, u32[]{:S(2)}) %collective-permute-start.127) | collective-permute-done | bytes 131104 | tf_op jit(solution)/shard_map/ppermute | solution.py:78
  84.4 0.1 maximum_select_fusion.1
  84.5 0.1 collective-permute-start.128
  84.6 1.5 %collective-permute-done.128 = bf16[64,2048]{1,0:T(8,128)(2,1)S(1)} collective-permute-done((bf16[64,2048]{1,0:T(8,128)(2,1)S(1)}, bf16[64,2048]{1,0:T(8,128)(2,1)S(1)}, u32[]{:S(2)}, u32[]{:S(2)}) %collective-permute-start.128) | collective-permute-done | bytes 262176 | tf_op jit(solution)/shard_map/ppermute | solution.py:78
  86.1 0.9 %maximum_select_fusion = bf16[1,64,4096]{2,1,0:T(8,128)(2,1)} fusion(bf16[1,64,2048]{2,1,0:T(8,128)(2,1)S(1)} %bitcast.3, bf16[1,64,2048]{2,1,0:T(8,128)(2,1)S(1)} %bitcast.4, pred[]{:T(512)S(6)} %eq.8), kind=kLoop, calls=%fused_computation | loop fusion | flops 2359296 | bytes 1048577 | tf_op jit(solution)/shard_map/jit(_where)/select_n | solution.py:357
  (3 shorter events, 0.1 us)
Async XLA Ops:
  0.0 26.7 %copy-start.3 = (bf16[2,512,256]{2,1,0:T(8,128)(2,1)S(1)}, bf16[2,512,256]{2,1,0:T(8,128)(2,1)}, u32[]{:S(2)}) copy-start(bf16[2,512,256]{2,1,0:T(8,128)(2,1)} %refs_2_.5) | copy-start | bytes 1572868
  5.0 13.4 %collective-permute-start.32 = (bf16[384,512]{1,0:T(8,128)(2,1)S(1)}, bf16[384,512]{1,0:T(8,128)(2,1)}, u32[]{:S(2)}, u32[]{:S(2)}) collective-permute-start(bf16[384,512]{1,0:T(8,128)(2,1)S(1)} %get-tuple-element.166), channel_id=1, source_target_pairs={{0,16},{1,3},{2,18},{3,1},{16,0},{17,19},{18,2},{19,17},{4,20},{5,... | collective-permute-start | bytes 1179656 | tf_op jit(solution)/shard_map/cond/branch_8_fun/ppermute | solution.py:83
  8.1 10.3 %collective-permute-start.33 = (bf16[384,512]{1,0:T(8,128)(2,1)S(1)}, bf16[384,512]{1,0:T(8,128)(2,1)}, u32[]{:S(2)}, u32[]{:S(2)}) collective-permute-start(bf16[384,512]{1,0:T(8,128)(2,1)S(1)} %get-tuple-element.166), channel_id=1, source_target_pairs={{0,2},{1,17},{2,0},{3,19},{16,18},{17,1},{18,16},{19,3},{4,6},{5,2... | collective-permute-start | bytes 1179656 | tf_op jit(solution)/shard_map/cond/branch_8_fun/ppermute | solution.py:83
  9.6 8.8 %collective-permute-start.34 = (bf16[384,512]{1,0:T(8,128)(2,1)S(1)}, bf16[384,512]{1,0:T(8,128)(2,1)}, u32[]{:S(2)}, u32[]{:S(2)}) collective-permute-start(bf16[384,512]{1,0:T(8,128)(2,1)S(1)} %get-tuple-element.166), channel_id=1, source_target_pairs={{0,1},{1,0},{2,3},{3,2},{4,5},{5,4},{6,7},{7,6},{8,9},{9,8},{10,11... | collective-permute-start | bytes 1179656 | tf_op jit(solution)/shard_map/cond/branch_8_fun/ppermute | solution.py:78
  9.6 8.8 %collective-permute-start.35 = (bf16[512,128]{1,0:T(8,128)(2,1)S(1)}, bf16[512,128]{1,0:T(8,128)(2,1)}, u32[]{:S(2)}, u32[]{:S(2)}) collective-permute-start(bf16[512,128]{1,0:T(8,128)(2,1)S(1)} %get-tuple-element.167), channel_id=1, source_target_pairs={{0,4},{4,8},{8,0},{12,12},{1,5},{5,9},{9,1},{13,13},{2,6},{6,10},{... | collective-permute-start | bytes 393224 | tf_op jit(solution)/shard_map/cond/branch_8_fun/ppermute | solution.py:295
  18.6 8.1 %collective-permute-start.122 = (bf16[384,512]{1,0:T(8,128)(2,1)}, bf16[384,512]{1,0:T(8,128)(2,1)S(1)}, u32[]{:S(2)}, u32[]{:S(2)}) collective-permute-start(bf16[384,512]{1,0:T(8,128)(2,1)} %get-tuple-element.223.refs_0_), channel_id=1, source_target_pairs={{0,2},{1,17},{2,0},{3,19},{16,18},{17,1},{18,16},{19,3},{4,6},{5,2... | collective-permute-start | bytes 1179656 | tf_op jit(solution)/shard_map/ppermute | solution.py:83
  19.2 20.3 %collective-permute-start.120 = (bf16[384,512]{1,0:T(8,128)(2,1)}, bf16[384,512]{1,0:T(8,128)(2,1)S(1)}, u32[]{:S(2)}, u32[]{:S(2)}) collective-permute-start(bf16[384,512]{1,0:T(8,128)(2,1)} %get-tuple-element.223.refs_0_), channel_id=1, source_target_pairs={{0,1},{1,0},{2,3},{3,2},{4,5},{5,4},{6,7},{7,6},{8,9},{9,8},{10,11... | collective-permute-start | bytes 1179656 | tf_op jit(solution)/shard_map/ppermute | solution.py:78
  19.9 19.6 %collective-permute-start.121 = (bf16[384,512]{1,0:T(8,128)(2,1)}, bf16[384,512]{1,0:T(8,128)(2,1)S(1)}, u32[]{:S(2)}, u32[]{:S(2)}) collective-permute-start(bf16[384,512]{1,0:T(8,128)(2,1)} %get-tuple-element.224.refs_2_), channel_id=1, source_target_pairs={{0,1},{1,0},{2,3},{3,2},{4,5},{5,4},{6,7},{7,6},{8,9},{9,8},{10,11... | collective-permute-start | bytes 1179656 | tf_op jit(solution)/shard_map/ppermute | solution.py:78
  26.7 15.2 %collective-permute-start.123 = (bf16[384,512]{1,0:T(8,128)(2,1)S(1)}, bf16[384,512]{1,0:T(8,128)(2,1)S(1)}, u32[]{:S(2)}, u32[]{:S(2)}) collective-permute-start(bf16[384,512]{1,0:T(8,128)(2,1)S(1)} %collective-permute-done.122.refs_0_), channel_id=1, source_target_pairs={{0,1},{1,0},{2,3},{3,2},{4,5},{5,4},{6,7},{7,6},{8,9},{9,8},{10,11... | collective-permute-start | bytes 1179656 | tf_op jit(solution)/shard_map/ppermute | solution.py:78
  33.7 5.8 %copy-start = (bf16[2048,4096]{1,0:T(8,128)(2,1)}, bf16[2048,4096]{1,0:T(8,128)(2,1)S(1)}, u32[]{:S(2)}) copy-start(bf16[2048,4096]{1,0:T(8,128)(2,1)S(1)} %get-tuple-element.231.refs_1_) | copy-start | bytes 50331652
  45.0 7.9 %collective-permute-start.104 = (bf16[64,1024]{1,0:T(8,128)(2,1)S(1)}, bf16[64,1024]{1,0:T(8,128)(2,1)}, u32[]{:S(2)}, u32[]{:S(2)}) collective-permute-start(bf16[64,1024]{1,0:T(8,128)(2,1)S(1)} %param.32), channel_id=1, source_target_pairs={{4,0},{8,4},{0,8},{12,12},{5,1},{9,5},{1,9},{13,13},{6,2},{10,6},{... | collective-permute-start | bytes 393224 | tf_op jit(solution)/shard_map/cond/branch_8_fun/ppermute | solution.py:71
  52.9 9.8 %collective-permute-start.124 = (bf16[64,1024]{1,0:T(8,128)(2,1)}, bf16[64,1024]{1,0:T(8,128)(2,1)S(1)}, u32[]{:S(2)}, u32[]{:S(2)}) collective-permute-start(bf16[64,1024]{1,0:T(8,128)(2,1)} %get-tuple-element.328.refs_0_), channel_id=1, source_target_pairs={{0,16},{16,0},{1,17},{17,1},{2,18},{18,2},{3,19},{19,3},{4,20},{20... | collective-permute-start | bytes 393224 | tf_op jit(solution)/shard_map/ppermute | solution.py:78
  54.5 5.8 %copy-start.1 = (bf16[2048,4096]{1,0:T(8,128)(2,1)S(1)}, bf16[2048,4096]{1,0:T(8,128)(2,1)}, u32[]{:S(2)}) copy-start(bf16[2048,4096]{1,0:T(8,128)(2,1)} %copy-done) | copy-start | bytes 50331652
  63.6 6.7 %collective-permute-start.125 = (f32[64,2048]{1,0:T(8,128)S(1)}, f32[64,2048]{1,0:T(8,128)S(1)}, u32[]{:S(2)}, u32[]{:S(2)}) collective-permute-start(f32[64,2048]{1,0:T(8,128)S(1)} %project_sent.1), channel_id=1, source_target_pairs={{0,1},{1,0},{2,3},{3,2},{4,5},{5,4},{6,7},{7,6},{8,9},{9,8},{10,11... | collective-permute-start | bytes 1572872 | tf_op jit(solution)/shard_map/ppermute | solution.py:78
  63.7 5.8 %copy-start.2 = (bf16[2048,4096]{1,0:T(8,128)(2,1)S(1)}, bf16[2048,4096]{1,0:T(8,128)(2,1)}, u32[]{:S(2)}) copy-start(bf16[2048,4096]{1,0:T(8,128)(2,1)} %copy-done) | copy-start | bytes 50331652
  70.4 8.8 %collective-permute-start.126 = (f32[64,1024]{1,0:T(8,128)S(1)}, f32[64,1024]{1,0:T(8,128)S(1)}, u32[]{:S(2)}, u32[]{:S(2)}) collective-permute-start(f32[64,1024]{1,0:T(8,128)S(1)} %slice_select_fusion), channel_id=1, source_target_pairs={{0,2},{1,3},{2,0},{3,1},{4,6},{5,7},{6,4},{7,5},{8,10},{9,11},{10,... | collective-permute-start | bytes 786440 | tf_op jit(solution)/shard_map/ppermute | solution.py:78
  79.2 5.2 %collective-permute-start.127 = (bf16[64,1024]{1,0:T(8,128)(2,1)S(1)}, bf16[64,1024]{1,0:T(8,128)(2,1)S(1)}, u32[]{:S(2)}, u32[]{:S(2)}) collective-permute-start(bf16[64,1024]{1,0:T(8,128)(2,1)S(1)} %add_convert_fusion), channel_id=1, source_target_pairs={{0,2},{1,3},{2,0},{3,1},{4,6},{5,7},{6,4},{7,5},{8,10},{9,11},{10,... | collective-permute-start | bytes 393224 | tf_op jit(solution)/shard_map/ppermute | solution.py:78
  84.5 1.6 %collective-permute-start.128 = (bf16[64,2048]{1,0:T(8,128)(2,1)S(1)}, bf16[64,2048]{1,0:T(8,128)(2,1)S(1)}, u32[]{:S(2)}, u32[]{:S(2)}) collective-permute-start(bf16[64,2048]{1,0:T(8,128)(2,1)S(1)} %maximum_select_fusion.1), channel_id=1, source_target_pairs={{0,1},{1,0},{2,3},{3,2},{4,5},{5,4},{6,7},{7,6},{8,9},{9,8},{10,11... | collective-permute-start | bytes 786440 | tf_op jit(solution)/shard_map/ppermute | solution.py:78
